TPU v7x, 32 devices: a whole 2x2x4 slice. The times are simulated.
32 devices in a mesh: table: 16 (over z, y, x), seq: 2 (over core).
Axes of the slice: x: 2, y: 2, z: 4, core: 2. Of those that a mesh axis runs over, the one named last changes fastest.
Arguments:
- embed_table: bfloat16 [131072, 512], P('table')
- lookup_ids: int32 [16, 2, 16, 192], P('table', 'seq'), may hold values from 0 to 8191
- counts: int32 [16, 2, 16], P('table', 'seq'), may hold values from 0 to 192, as said below
- event_order: int32 [16, 2, 2048], P('table', 'seq'), may hold values from 0 to 2047, each once within a row
- hist_len: int32 [16], P('table'), may hold values from 1024 to 4096, as said below
- w_uvqk: bfloat16 [512, 2048], replicated, may hold values from -0.25 to 0.25
- w_out: bfloat16 [512, 512], replicated, may hold values from -0.25 to 0.25
Outputs:
- layer_out: bfloat16 [16, 4096, 512], P('table', 'seq')
Inputs may be any that keep to these rules, and one draw needn't show every extreme that they name: For every user and piece the 16 counts sum to 2048; for every piece index one shard gets exactly 192 from every user. Only the first counts[u, p, j] slots of lookup_ids[u, p, j] are read. `hist_len`: some user has exactly 4096 events.
All inputs are finite; a program needn't handle non-finite values.
Results may differ from a plain program's by a relative error of at most 0.0039.
Values may be sent and summed in bfloat16 or wider, within the bound.
A program may use at most 128 MiB of HBM per device.

v0:
```python
import jax
import jax.numpy as jnp
from jax import lax
from jax.sharding import PartitionSpec as P

HEADS = 4
WINDOW = 1024


def passed_along(value, axis, steps):
    count = lax.axis_size(axis)
    initial, last = (max(0, -steps), min(count, count - steps))
    return lax.ppermute(value, axis, [(source, source + steps) for source in range(initial, last)])


def normalize(values):
    average = jnp.mean(values, axis=-1, keepdims=True)
    centered = values - average
    spread = jnp.mean(centered * centered, axis=-1, keepdims=True)
    return centered * lax.rsqrt(spread + 1e-05)


def attend_block(queries, keyvals, head_count):
    query_rows, width = queries.shape
    key_rows = keyvals.shape[0]
    head_width = width // head_count
    query_heads = queries.reshape(query_rows, head_count, head_width)
    key_heads = keyvals[:, :width].reshape(key_rows, head_count, head_width)
    value_heads = keyvals[:, width:].reshape(key_rows, head_count, head_width)
    scores = jnp.einsum("qhd,khd->hqk", query_heads, key_heads, preferred_element_type=jnp.float32)
    scores = scores * head_width ** (-0.5)
    distance = (
        jnp.arange(query_rows)[:, None] + (key_rows - query_rows) - jnp.arange(key_rows)[None, :]
    )
    inside = (distance >= 0) & (distance < key_rows - query_rows)
    weights = jnp.where(inside[None], jax.nn.silu(scores), 0.0).astype(jnp.bfloat16)
    attended = jnp.einsum("hqk,khd->qhd", weights, value_heads, preferred_element_type=jnp.float32)
    return attended.reshape(query_rows, width)


def local(embed_table, lookup_ids, counts, event_order, hist_len, w_uvqk, w_out):
    shards = lax.axis_size("table")
    capacity = lookup_ids.shape[3]
    tokens = event_order.shape[2]
    width = embed_table.shape[1]
    requests = lookup_ids[0, 0]
    fetched = lax.all_to_all(
        embed_table[lax.all_to_all(requests, "table", split_axis=0, concat_axis=0, tiled=True)],
        "table",
        split_axis=0,
        concat_axis=0,
        tiled=True,
    )
    live_counts = counts[0, 0]
    totals = jnp.cumsum(live_counts)
    starts = totals - live_counts
    event_rank = event_order[0, 0]
    owner_shard = jnp.sum((event_rank[:, None] >= totals[None, :]).astype(jnp.int32), axis=1)
    chosen = owner_shard[:, None] == jnp.arange(shards, dtype=jnp.int32)[None, :]
    slot_start = jnp.sum(jnp.where(chosen, starts[None, :], 0), axis=1)
    slot_index = owner_shard * capacity + event_rank - slot_start
    events = fetched.reshape(shards * capacity, width)[slot_index]
    normed = normalize(events.astype(jnp.float32)).astype(jnp.bfloat16)
    activated = jax.nn.silu(jnp.dot(normed, w_uvqk, preferred_element_type=jnp.float32)).astype(
        jnp.bfloat16
    )
    gate_part = activated[:, :width]
    queries = activated[:, width : 2 * width]
    keyvals = activated[:, 2 * width :]
    before = passed_along(keyvals[tokens - WINDOW :], "seq", 1)
    context = jnp.concatenate([before, keyvals], axis=0)
    blocks = []
    for block_index in range(tokens // WINDOW):
        first = block_index * WINDOW
        blocks.append(
            attend_block(
                queries[first : first + WINDOW], context[first : first + 2 * WINDOW], HEADS
            )
        )
    attended = jnp.concatenate(blocks, axis=0)
    gated_rows = (normalize(attended) * gate_part.astype(jnp.float32)).astype(jnp.bfloat16)
    result = jnp.dot(gated_rows, w_out, preferred_element_type=jnp.float32) + events.astype(
        jnp.float32
    )
    position = lax.axis_index("seq") * tokens + jnp.arange(tokens, dtype=jnp.int32)
    result = jnp.where((position < hist_len[0])[:, None], result, 0.0)
    return result.astype(jnp.bfloat16)[None]


def solution(mesh):
    in_specs = (
        P("table", None),
        P("table", "seq", None, None),
        P("table", "seq", None),
        P("table", "seq", None),
        P("table"),
        P(),
        P(),
    )
    out_specs = P("table", "seq", None)
    return jax.shard_map(local, mesh=mesh, in_specs=in_specs, out_specs=out_specs, check_vma=False)
```

profile of v0, /device:TPU:16, one launch (start us, length us, event | category | flops | bytes accessed | tf_op | source)
XLA Modules:
  0.0 194.5 jit_solution(3509435219938681349)
XLA Ops:
  0.0 0.0 copy-start
  0.0 0.9 all_to_all.11
  0.9 12.0 %all_to_all.17 = s32[16,1,192]{2,1,0:T(1,128)S(1)} all-to-all(s32[16,1,192]{2,1,0:T(1,128)S(1)} %all_to_all.11), channel_id=1, replica_groups=mesh['table'=16,'seq'=2] {'table'}, dimensions={0} | all-to-all | bytes 24576 | tf_op jit(solution)/shard_map/all_to_all | solution.py:48
  12.9 0.1 fusion.22
  13.0 0.1 reshape.192
  13.0 17.8 %gather_fusion = bf16[3072,512]{1,0:T(8,128)(2,1)} fusion(bf16[8192,512]{1,0:T(8,128)(2,1)} %param.7, s32[3072]{0:T(1024)S(1)} %broadcast_clamp_fusion), kind=kCustom, calls=%fused_computation | custom fusion | bytes 6303744 | tf_op jit(solution)/shard_map/gather | solution.py:48
  30.8 0.0 copy-start.8
  30.8 0.0 copy-start.6
  30.8 6.7 %all-to-all-start.1 = ((bf16[16,192,512]{2,1,0:T(8,128)(2,1)}), bf16[16,192,512]{2,1,0:T(8,128)(2,1)}, u32[]{:S(2)}, u32[]{:S(2)}) async-start(bf16[16,192,512]{2,1,0:T(8,128)(2,1)} %bitcast.43), calls=%async_computation.1 | async-start | bytes 6291456 | tf_op jit(solution)/shard_map/all_to_all | solution.py:47
  37.5 0.0 copy-done.8
  37.5 0.1 copy.23
  37.6 0.1 reduce.1
  38.4 0.6 add_compare_fusion
  39.0 0.0 copy-done.6
  39.0 0.1 convert_reduce_fusion.1
  39.1 0.1 select_reduce_fusion
  39.3 3.7 %fusion.2 = pred[1024,2048]{1,0:T(8,128)(4,1)} fusion(s32[1024]{0:T(1024)S(1)} %iota_add_fusion), kind=kLoop, calls=%fused_computation.8 | loop fusion | flops 8388608 | bytes 2101248 | tf_op jit(solution)/shard_map/and | solution.py:35
  43.0 63.7 %all-to-all-done.1 = bf16[16,192,512]{2,1,0:T(8,128)(2,1)} async-done(((bf16[16,192,512]{2,1,0:T(8,128)(2,1)}), bf16[16,192,512]{2,1,0:T(8,128)(2,1)}, u32[]{:S(2)}, u32[]{:S(2)}) %all-to-all-start.1) | async-done | bytes 3145760 | tf_op jit(solution)/shard_map/all_to_all | solution.py:47
  106.7 11.6 %gather_fusion.1 = bf16[2048,512]{1,0:T(8,128)(2,1)} fusion(bf16[3072,512]{1,0:T(8,128)(2,1)} %bitcast.3, s32[2048]{0:T(1024)S(1)} %broadcast_clamp_fusion.1), kind=kCustom, calls=%fused_computation.1 | custom fusion | bytes 4202496 | tf_op jit(solution)/shard_map/gather | solution.py:62
  118.2 0.0 copy-start.1
  118.2 2.1 %convert_reduce_fusion = f32[2048]{0:T(1024)S(1)} fusion(bf16[2048,512]{1,0:T(8,128)(2,1)} %gather_fusion.1), kind=kLoop, calls=%fused_computation.11 | loop fusion | flops 2095104 | bytes 2105344 | tf_op jit(solution)/shard_map/reduce_sum | solution.py:17
  120.3 2.5 %fusion.7 = f32[2048]{0:T(1024)S(1)} fusion(bf16[2048,512]{1,0:T(8,128)(2,1)} %gather_fusion.1, f32[2048]{0:T(1024)S(1)} %broadcast_multiply_fusion.1), kind=kLoop, calls=%fused_computation.16 | loop fusion | flops 4192256 | bytes 2113536 | tf_op jit(solution)/shard_map/reduce_sum | solution.py:19
  122.8 0.0 copy-done
  122.8 0.0 copy-done.1
  122.9 8.8 %multiply_convert_fusion = bf16[2048,2048]{0,1:T(8,128)(2,1)S(1)} fusion(bf16[512,2048]{1,0:T(8,128)(2,1)S(1)} %copy-done, bf16[2048,512]{1,0:T(8,128)(2,1)S(1)} %copy-done.1, f32[2048]{0:T(1024)S(1)} %add_rsqrt_fusion.1, f32[2048]{0:T(1024)S(1)} %broadcast_multiply_fusion.1), kind=kOutput, calls=%fused_computation.4 | convolution fusion | flops 4320133120 | bytes 12599296 | tf_op jit(solution)/shard_map/dot_general | solution.py:64
  131.7 0.0 copy-start.3
  131.7 1.8 slice.49
  133.5 1.9 fusion.31
  135.3 0.6 copy-done.3
  135.9 2.2 %fusion.32 = (bf16[2048,512]{0,1:T(8,128)(2,1)}, bf16[2048,512]{0,1:T(8,128)(2,1)}) fusion(bf16[2048,2048]{0,1:T(8,128)(2,1)S(1)} %multiply_convert_fusion), kind=kLoop, calls=%fused_computation.59 | loop fusion | bytes 8388608 | tf_op jit(solution)/shard_map/slice | solution.py:28
  138.1 2.6 %collective-permute-start = (bf16[1024,1024]{0,1:T(8,128)(2,1)}, bf16[1024,1024]{0,1:T(8,128)(2,1)}, u32[]{:S(2)}, u32[]{:S(2)}) collective-permute-start(bf16[1024,1024]{0,1:T(8,128)(2,1)} %slice.49), channel_id=1, source_target_pairs={{0,1},{2,3},{4,5},{6,7},{8,9},{10,11},{12,13},{14,15},{16,17},{18,... | collective-permute-start | bytes 6291464 | tf_op jit(solution)/shard_map/ppermute | solution.py:13
  140.8 19.6 %fusion.4 = f32[4,128,1024]{2,1,0:T(8,128)} fusion(bf16[2048,4,128]{0,2,1:T(8,128)(2,1)} %bitcast.53, bf16[1024,4,128]{0,2,1:T(8,128)(2,1)} %bitcast.55, bf16[2048,4,128]{0,2,1:T(8,128)(2,1)} %bitcast.52, pred[1024,2048]{1,0:T(8,128)(4,1)} %fusion.2), kind=kOutput, calls=%fused_computation.13 | convolution fusion | flops 4353687552 | bytes 9437184 | tf_op jit(solution)/shard_map/hqk,khd->qhd/dot_general | solution.py:37
  160.3 0.0 slice-start
  160.3 0.0 collective-permute-done
  160.3 2.2 %slice-done = bf16[2048,1024]{0,1:T(8,128)(2,1)S(1)} async-done(((bf16[2048,2048]{0,1:T(8,128)(2,1)}), bf16[2048,1024]{0,1:T(8,128)(2,1)S(1)}, s32[]{:S(2)}) %slice-start) | async-done | bytes 4194328 | tf_op jit(solution)/shard_map/slice | solution.py:69
  162.5 4.0 %pad_maximum_fusion.1 = (bf16[2048,512]{0,1:T(8,128)(2,1)}, bf16[2048,512]{0,1:T(8,128)(2,1)}) fusion(bf16[2048,1024]{0,1:T(8,128)(2,1)S(1)} %slice-done, bf16[1024,1024]{0,1:T(8,128)(2,1)} %collective-permute-done), kind=kLoop, calls=%fused_computation.27 | loop fusion | flops 8388608 | bytes 10485760 | tf_op jit(solution)/shard_map/concatenate | solution.py:71
  166.6 19.3 %fusion.3 = f32[4,128,1024]{2,1,0:T(8,128)} fusion(bf16[2048,4,128]{0,2,1:T(8,128)(2,1)} %bitcast.51, bf16[1024,4,128]{0,2,1:T(8,128)(2,1)S(1)} %bitcast.54, bf16[2048,4,128]{0,2,1:T(8,128)(2,1)} %bitcast.50, pred[1024,2048]{1,0:T(8,128)(4,1)} %fusion.2), kind=kOutput, calls=%fused_computation.12 | convolution fusion | flops 4353687552 | bytes 9437184 | tf_op jit(solution)/shard_map/hqk,khd->qhd/dot_general | solution.py:37
  185.8 0.0 copy-start.4
  185.8 0.0 copy-start.7
  185.8 0.0 copy-start.9
  185.9 2.6 %fusion.12 = f32[2048]{0:T(1024)S(1)} fusion(f32[1024,512]{0,1:T(8,128)} %bitcast.44, f32[1024,512]{0,1:T(8,128)} %bitcast.47), kind=kLoop, calls=%fused_computation.24 | loop fusion | flops 2095104 | bytes 4202496 | tf_op jit(solution)/shard_map/reduce_sum | solution.py:17
  188.5 0.2 copy-done.4
  188.7 0.6 copy-done.5
  189.3 0.5 multiply_reduce_fusion
  189.8 0.1 copy-done.2
  189.9 0.0 copy-done.7
  189.9 0.0 copy-done.9
  190.0 4.5 %fusion.11 = bf16[1,2048,512]{2,1,0:T(8,128)(2,1)} fusion(bf16[2048,512]{1,0:T(8,128)(2,1)S(1)} %copy-done.2, bf16[512,512]{1,0:T(8,128)(2,1)S(1)} %copy-done.9, f32[1024,512]{0,1:T(8,128)S(1)} %bitcast.46, f32[1024,512]{0,1:T(8,128)S(1)} %bitcast.49, bf16[2048,2048]{0,1:T(8,128)(2,1)} %copy-done.3, f32[2048]{0:T(1024)S(1)} %add_rsqrt_fusion, ...), kind=kOutput, calls=%fused_computation.23 | convolution fusion | flops 1084227584 | bytes 11028480 | tf_op jit(solution)/shard_map/dot_general | solution.py:82
  (13 shorter events, 0.1 us)
Async XLA Ops:
  0.0 122.8 %copy-start = (bf16[512,2048]{1,0:T(8,128)(2,1)S(1)}, bf16[512,2048]{1,0:T(8,128)(2,1)}, u32[]{:S(2)}) copy-start(bf16[512,2048]{1,0:T(8,128)(2,1)} %param.12) | copy-start | bytes 6291460
  30.8 6.7 %copy-start.8 = (s32[1,1,16]{2,1,0:T(1,128)S(1)}, s32[1,1,16]{2,1,0:T(1,128)}, u32[]{:S(2)}) copy-start(s32[1,1,16]{2,1,0:T(1,128)} %param.9) | copy-start | bytes 196
  30.8 8.2 %copy-start.6 = (s32[1,1,2048]{2,1,0:T(1,128)S(1)}, s32[1,1,2048]{2,1,0:T(1,128)}, u32[]{:S(2)}) copy-start(s32[1,1,2048]{2,1,0:T(1,128)} %param.10) | copy-start | bytes 24580
  30.8 75.9 %all-to-all-start.1 = ((bf16[16,192,512]{2,1,0:T(8,128)(2,1)}), bf16[16,192,512]{2,1,0:T(8,128)(2,1)}, u32[]{:S(2)}, u32[]{:S(2)}) async-start(bf16[16,192,512]{2,1,0:T(8,128)(2,1)} %bitcast.43), calls=%async_computation.1 | async-start | bytes 6291456 | tf_op jit(solution)/shard_map/all_to_all | solution.py:47
  118.2 4.6 %copy-start.1 = (bf16[2048,512]{1,0:T(8,128)(2,1)S(1)}, bf16[2048,512]{1,0:T(8,128)(2,1)}, u32[]{:S(2)}) copy-start(bf16[2048,512]{1,0:T(8,128)(2,1)} %gather_fusion.1) | copy-start | bytes 6291460
  131.7 4.2 %copy-start.3 = (bf16[2048,2048]{0,1:T(8,128)(2,1)}, bf16[2048,2048]{0,1:T(8,128)(2,1)S(1)}, u32[]{:S(2)}) copy-start(bf16[2048,2048]{0,1:T(8,128)(2,1)S(1)} %multiply_convert_fusion) | copy-start | bytes 25165828
  138.1 22.2 %collective-permute-start = (bf16[1024,1024]{0,1:T(8,128)(2,1)}, bf16[1024,1024]{0,1:T(8,128)(2,1)}, u32[]{:S(2)}, u32[]{:S(2)}) collective-permute-start(bf16[1024,1024]{0,1:T(8,128)(2,1)} %slice.49), channel_id=1, source_target_pairs={{0,1},{2,3},{4,5},{6,7},{8,9},{10,11},{12,13},{14,15},{16,17},{18,... | collective-permute-start | bytes 6291464 | tf_op jit(solution)/shard_map/ppermute | solution.py:13
  160.3 2.2 %slice-start = ((bf16[2048,2048]{0,1:T(8,128)(2,1)}), bf16[2048,1024]{0,1:T(8,128)(2,1)S(1)}, s32[]{:S(2)}) async-start(bf16[2048,2048]{0,1:T(8,128)(2,1)} %copy-done.3), calls=%async_computation.2 | async-start | bytes 8388608 | tf_op jit(solution)/shard_map/slice | solution.py:69
  185.8 2.9 %copy-start.4 = (f32[4,128,1024]{2,1,0:T(8,128)S(1)}, f32[4,128,1024]{2,1,0:T(8,128)}, u32[]{:S(2)}) copy-start(f32[4,128,1024]{2,1,0:T(8,128)} %fusion.4) | copy-start | bytes 6291460
  185.8 3.5 %copy-start.5 = (f32[4,128,1024]{2,1,0:T(8,128)S(1)}, f32[4,128,1024]{2,1,0:T(8,128)}, u32[]{:S(2)}) copy-start(f32[4,128,1024]{2,1,0:T(8,128)} %fusion.3) | copy-start | bytes 6291460
  185.8 4.1 %copy-start.2 = (bf16[2048,512]{1,0:T(8,128)(2,1)S(1)}, bf16[2048,512]{1,0:T(8,128)(2,1)}, u32[]{:S(2)}) copy-start(bf16[2048,512]{1,0:T(8,128)(2,1)} %gather_fusion.1) | copy-start | bytes 6291460
  185.8 4.1 %copy-start.7 = (pred[2048]{0:T(1024)(128)(4,1)S(1)}, pred[2048]{0:T(1024)(128)(4,1)}, u32[]{:S(2)}) copy-start(pred[2048]{0:T(1024)(128)(4,1)} %add_compare_fusion) | copy-start | bytes 6148
  185.8 4.2 %copy-start.9 = (bf16[512,512]{1,0:T(8,128)(2,1)S(1)}, bf16[512,512]{1,0:T(8,128)(2,1)}, u32[]{:S(2)}) copy-start(bf16[512,512]{1,0:T(8,128)(2,1)} %param.13) | copy-start | bytes 1572868
where the time goes:
time: 196 us; the launch traced here: 195 us
  waiting for transfers between devices  63.7 us (32%)
  matrix products  52.2 us (27%)
  local copies, waits for them, and re-layouts  40 us (20%)
  other arithmetic  16.5 us (8%)
  blocking collectives  12 us (6%)
  starting transfers between devices  9.33 us (5%)
    all_to_all x1, waiting for transfers between devices, local(): lax.all_to_all(embed_table[lax.all_to_all(requests, 'table', split_axis=0...  63.7 us
    dot_general x2, matrix products, attend_block(): jnp.einsum('hqk,khd->qhd', weights, value_heads, preferred_element_type=j...  38.8 us
    gather x1, local copies, waits for them, and re-layouts, local(): embed_table[lax.all_to_all(requests, 'table', split_axis=0, concat_axis=0...  17.8 us
    all_to_all x1, blocking collectives, local(): lax.all_to_all(requests, 'table', split_axis=0, concat_axis=0, tiled=True)  12 us
    gather x1, local copies, waits for them, and re-layouts, local(): events = fetched.reshape(shards * capacity, width)[slot_index]  11.6 us
    dot_general x1, matrix products, local(): jnp.dot(normed, w_uvqk, preferred_element_type=jnp.float32)  8.83 us
    all_to_all x1, starting transfers between devices, local(): lax.all_to_all(embed_table[lax.all_to_all(requests, 'table', split_axis=0...  6.71 us
    reduce_sum x2, other arithmetic, normalize(): average = jnp.mean(values, axis=-1, keepdims=True)  4.69 us
  transfers between devices with their start and end apart: 2, of which 1 were waited for; matrix products, arithmetic and copies ran while one was open for 13% of the time, Pallas kernels for 0%

commit v1 on v0

v1 whole, which is shorter than its diff:
```python
import functools

import jax
import jax.numpy as jnp
from jax import lax
from jax.experimental import pallas as pl
from jax.experimental.pallas import tpu as pltpu
from jax.sharding import PartitionSpec as P

HEADS = 4
WINDOW = 1024
BLOCK = 256
VMEM_LIMIT = 48 * 1024 * 1024


def passed_along(value, axis, steps):
    count = lax.axis_size(axis)
    initial, last = (max(0, -steps), min(count, count - steps))
    return lax.ppermute(value, axis, [(source, source + steps) for source in range(initial, last)])


def normalize(values):
    average = jnp.mean(values, axis=-1, keepdims=True)
    centered = values - average
    spread = jnp.mean(centered * centered, axis=-1, keepdims=True)
    return centered * lax.rsqrt(spread + 1e-05)


def silu_of_double(half):
    return half + half * jnp.tanh(half)


def project_kernel(query_scale, events_ref, w_ref, gate_ref, query_ref, keyval_ref):
    width = events_ref.shape[1]
    normed = normalize(events_ref[...].astype(jnp.float32)).astype(jnp.bfloat16)

    def columns(first, count):
        product = jnp.dot(normed, w_ref[:, first : first + count], preferred_element_type=jnp.float32)
        return silu_of_double(0.5 * product)

    gate_ref[...] = columns(0, width).astype(gate_ref.dtype)
    query_ref[...] = (columns(width, width) * query_scale).astype(query_ref.dtype)
    keyval_ref[:, :width] = columns(2 * width, width).astype(keyval_ref.dtype)
    keyval_ref[:, width:] = columns(3 * width, width).astype(keyval_ref.dtype)


def project(events, w_uvqk):
    tokens, width = events.shape
    rows = 512
    query_scale = 0.5 * (width // HEADS) ** (-0.5)
    kind = jnp.bfloat16
    return pl.pallas_call(
        functools.partial(project_kernel, query_scale),
        grid=(tokens // rows,),
        in_specs=[
            pl.BlockSpec((rows, width), lambda i: (i, 0)),
            pl.BlockSpec((width, 4 * width), lambda i: (0, 0)),
        ],
        out_specs=[
            pl.BlockSpec((rows, width), lambda i: (i, 0)),
            pl.BlockSpec((rows, width), lambda i: (i, 0)),
            pl.BlockSpec((rows, 2 * width), lambda i: (i, 0)),
        ],
        out_shape=[
            jax.ShapeDtypeStruct((tokens, width), kind),
            jax.ShapeDtypeStruct((tokens, width), kind),
            jax.ShapeDtypeStruct((tokens, 2 * width), kind),
        ],
        compiler_params=pltpu.CompilerParams(vmem_limit_bytes=VMEM_LIMIT),
        cost_estimate=pl.CostEstimate(
            flops=8 * tokens * width * width,
            bytes_accessed=10 * tokens * width + 8 * width * width,
            transcendentals=4 * tokens * width,
        ),
        name="project",
    )(events, w_uvqk)


def scores_of(queries, keys):
    return lax.dot_general(
        queries, keys, (((1,), (1,)), ((), ())), preferred_element_type=jnp.float32
    )


def attend_kernel(live_ref, query_ref, before_ref, own_ref, gate_ref, events_ref, w_ref, *rest):
    out_ref, context, heads_out = rest[-3:]
    rows, width = query_ref.shape
    head_width = width // HEADS
    block = pl.program_id(0)

    @pl.when(block == 0)
    def _():
        context[:WINDOW] = before_ref[...]
        context[WINDOW:] = own_ref[...]

    row = lax.broadcasted_iota(jnp.int32, (rows, rows), 0)
    column = lax.broadcasted_iota(jnp.int32, (rows, rows), 1)
    near = column <= row
    near_weight = near.astype(jnp.float32).astype(jnp.bfloat16)
    first = pl.multiple_of(block * rows, rows)
    far_rows = pl.ds(first, rows)
    middle_rows = pl.ds(pl.multiple_of(first + rows, rows), WINDOW - rows)
    near_rows = pl.ds(pl.multiple_of(first + WINDOW, rows), rows)
    for head in range(HEADS):
        at = slice(head * head_width, (head + 1) * head_width)
        value_at = slice(width + head * head_width, width + (head + 1) * head_width)
        queries = query_ref[:, at]
        edge = jnp.where(
            near,
            scores_of(queries, context[near_rows, at]),
            scores_of(queries, context[far_rows, at]),
        )
        edge = silu_of_double(edge.astype(jnp.bfloat16))
        edge_near = edge * near_weight
        edge_far = edge - edge_near
        middle = scores_of(queries, context[middle_rows, at]).astype(jnp.bfloat16)
        middle = silu_of_double(middle)
        total = jnp.dot(middle, context[middle_rows, value_at], preferred_element_type=jnp.float32)
        total += jnp.dot(edge_near, context[near_rows, value_at], preferred_element_type=jnp.float32)
        total += jnp.dot(edge_far, context[far_rows, value_at], preferred_element_type=jnp.float32)
        heads_out[:, at] = total
    gated = normalize(heads_out[...]) * gate_ref[...].astype(jnp.float32)
    result = jnp.dot(gated.astype(jnp.bfloat16), w_ref[...], preferred_element_type=jnp.float32)
    result = result + events_ref[...].astype(jnp.float32)
    position = first + lax.broadcasted_iota(jnp.int32, (rows, 1), 0)
    out_ref[...] = jnp.where(position < live_ref[0], result, 0.0).astype(out_ref.dtype)


def attend(part, live, queries, before, keyvals, gate, events, w_out, partial_out):
    tokens, width = events.shape
    per_part = WINDOW // BLOCK
    rowed = pl.BlockSpec((BLOCK, width), lambda i: (part * per_part + i, 0))
    if before is None:
        before = keyvals
        before_spec = pl.BlockSpec((WINDOW, 2 * width), lambda i: (part - 1, 0))
    else:
        before_spec = pl.BlockSpec((WINDOW, 2 * width), lambda i: (0, 0))
    operands = [live, queries, before, keyvals, gate, events, w_out]
    in_specs = [
        pl.BlockSpec(memory_space=pltpu.SMEM),
        rowed,
        before_spec,
        pl.BlockSpec((WINDOW, 2 * width), lambda i: (part, 0)),
        rowed,
        rowed,
        pl.BlockSpec((width, width), lambda i: (0, 0)),
    ]
    aliases = {}
    if partial_out is not None:
        aliases = {len(operands): 0}
        operands.append(partial_out)
        in_specs.append(pl.BlockSpec(memory_space=pl.ANY))
    return pl.pallas_call(
        attend_kernel,
        grid=(per_part,),
        in_specs=in_specs,
        out_specs=rowed,
        out_shape=jax.ShapeDtypeStruct((tokens, width), jnp.bfloat16),
        scratch_shapes=[
            pltpu.VMEM((2 * WINDOW, 2 * width), jnp.bfloat16),
            pltpu.VMEM((BLOCK, width), jnp.float32),
        ],
        input_output_aliases=aliases,
        compiler_params=pltpu.CompilerParams(vmem_limit_bytes=VMEM_LIMIT),
        cost_estimate=pl.CostEstimate(
            flops=4 * WINDOW * (WINDOW + BLOCK) * width + 2 * WINDOW * width * width,
            bytes_accessed=16 * WINDOW * width + 2 * width * width,
            transcendentals=WINDOW * WINDOW * HEADS,
        ),
        name="attend",
    )(*operands)


def look_up(embed_table, lookup_ids, counts, event_order):
    shards = lax.axis_size("table")
    capacity = lookup_ids.shape[3]
    width = embed_table.shape[1]
    requests = lookup_ids[0, 0]
    fetched = lax.all_to_all(
        embed_table[lax.all_to_all(requests, "table", split_axis=0, concat_axis=0, tiled=True)],
        "table",
        split_axis=0,
        concat_axis=0,
        tiled=True,
    )
    live_counts = counts[0, 0]
    totals = jnp.cumsum(live_counts)
    starts = totals - live_counts
    event_rank = event_order[0, 0]
    owner_shard = jnp.sum((event_rank[:, None] >= totals[None, :]).astype(jnp.int32), axis=1)
    chosen = owner_shard[:, None] == jnp.arange(shards, dtype=jnp.int32)[None, :]
    slot_start = jnp.sum(jnp.where(chosen, starts[None, :], 0), axis=1)
    slot_index = owner_shard * capacity + event_rank - slot_start
    return fetched.reshape(shards * capacity, width)[slot_index]


def local(embed_table, lookup_ids, counts, event_order, hist_len, w_uvqk, w_out):
    events = look_up(embed_table, lookup_ids, counts, event_order)
    tokens = events.shape[0]
    gate, queries, keyvals = project(events, w_uvqk)
    before = passed_along(keyvals[tokens - WINDOW :], "seq", 1)
    live = hist_len - lax.axis_index("seq") * tokens
    out = None
    for part in reversed(range(tokens // WINDOW)):
        out = attend(
            part,
            live - part * WINDOW,
            queries,
            before if part == 0 else None,
            keyvals,
            gate,
            events,
            w_out,
            out,
        )
    return out[None]


def solution(mesh):
    in_specs = (
        P("table", None),
        P("table", "seq", None, None),
        P("table", "seq", None),
        P("table", "seq", None),
        P("table"),
        P(),
        P(),
    )
    out_specs = P("table", "seq", None)
    return jax.shard_map(local, mesh=mesh, in_specs=in_specs, out_specs=out_specs, check_vma=False)
```

time: 196 us -> 158 us (0.81)
  matrix products: 52.2 us -> 0 us
  Pallas kernels: 0 us -> 33 us
  other arithmetic: 16.5 us -> 0.44 us
  local copies, waits for them, and re-layouts: 40 us -> 34 us
  waiting for transfers between devices: 63.7 us -> 68.5 us
    dot_general x4 -> x0, matrix products: 52.2 us -> none  [the longest x2 38.8 us: attend_block(): jnp.einsum('hqk,khd->qhd', weights, value_heads, preferred_element_type=j...]
    pallas_call x0 -> x3, Pallas kernels: none -> 33 us  [the longest x2 23 us: attend(): pl.pallas_call(attend_kernel, grid=(per_part,), in_specs=in_specs, out_sp...]
    reduce_sum x6 -> x2, other arithmetic: 7.88 us -> 0.19 us  [the longest x1 0.1 us: look_up(): jnp.sum((event_rank[:, None] >= totals[None, :]).astype(jnp.int32), axis=1)]
    slice x4 -> x0, local copies, waits for them, and re-layouts: 6.27 us -> none  [the longest x1 2.23 us: attend_block(): key_heads = keyvals[:, :width].reshape(key_rows, head_count, head_width)]
    all_to_all x1, waiting for transfers between devices: 63.7 us -> 68.5 us  [look_up(): lax.all_to_all(embed_table[lax.all_to_all(requests, 'table', split_axis=0...]
    concatenate x1 -> x0, other arithmetic: 4.04 us -> none  [local(): context = jnp.concatenate([before, keyvals], axis=0)]
    and x1 -> x0, other arithmetic: 3.73 us -> none  [attend_block(): inside = (distance >= 0) & (distance < key_rows - query_rows)]
    slice x1, local copies, waits for them, and re-layouts: 1.78 us -> 4.59 us  [local(): before = passed_along(keyvals[tokens - WINDOW:], 'seq', 1)]
  transfers between devices with their start and end apart: 2 -> 2, of which waited for: 1 -> 1; matrix products, arithmetic and copies ran while one was open for 13% -> 0% of each run, Pallas kernels for 0% -> 7%
where the time goes in v1:
time: 158 us; the launch traced here: 157 us
  waiting for transfers between devices  68.5 us (43%)
  local copies, waits for them, and re-layouts  34 us (22%)
  Pallas kernels  33 us (21%)
  blocking collectives  12 us (8%)
  starting transfers between devices  8.71 us (6%)
    all_to_all x1, waiting for transfers between devices, look_up(): lax.all_to_all(embed_table[lax.all_to_all(requests, 'table', split_axis=0...  68.5 us
    pallas_call x2, Pallas kernels, attend(): pl.pallas_call(attend_kernel, grid=(per_part,), in_specs=in_specs, out_sp...  23 us
    gather x1, local copies, waits for them, and re-layouts, look_up(): embed_table[lax.all_to_all(requests, 'table', split_axis=0, concat_axis=0...  17.8 us
    all_to_all x1, blocking collectives, look_up(): lax.all_to_all(requests, 'table', split_axis=0, concat_axis=0, tiled=True)  12 us
    pallas_call x1, Pallas kernels, project(): pl.pallas_call(functools.partial(project_kernel, query_scale), grid=(toke...  10.1 us
    gather x1, local copies, waits for them, and re-layouts, look_up(): return fetched.reshape(shards * capacity, width)[slot_index]  9.17 us
    all_to_all x1, starting transfers between devices, look_up(): lax.all_to_all(embed_table[lax.all_to_all(requests, 'table', split_axis=0...  6.03 us
    slice x1, local copies, waits for them, and re-layouts, local(): before = passed_along(keyvals[tokens - WINDOW:], 'seq', 1)  4.59 us
  transfers between devices with their start and end apart: 2, of which 1 were waited for; matrix products, arithmetic and copies ran while one was open for 0% of the time, Pallas kernels for 7%

profile of v1, /device:TPU:16, one launch (start us, length us, event | category | flops | bytes accessed | tf_op | source)
XLA Modules:
  0.0 157.5 jit_solution(3881493374970064641)
XLA Ops:
  0.0 0.7 all_to_all.11
  0.7 12.0 %all_to_all.17 = s32[16,1,192]{2,1,0:T(1,128)S(1)} all-to-all(s32[16,1,192]{2,1,0:T(1,128)S(1)} %all_to_all.11), channel_id=1, replica_groups=mesh['table'=16,'seq'=2] {'table'}, dimensions={0} | all-to-all | bytes 24576 | tf_op jit(solution)/shard_map/all_to_all | solution.py:180
  12.7 0.1 fusion
  12.8 0.1 reshape.104
  12.9 17.8 %gather_fusion = bf16[3072,512]{1,0:T(8,128)(2,1)} fusion(bf16[8192,512]{1,0:T(8,128)(2,1)} %param.7, s32[3072]{0:T(1024)S(1)} %broadcast_clamp_fusion), kind=kCustom, calls=%fused_computation | custom fusion | bytes 6303744 | tf_op jit(solution)/shard_map/gather | solution.py:180
  30.6 0.0 copy-start.5
  30.6 0.0 copy-start.4
  30.6 6.0 %all-to-all-start.1 = ((bf16[16,192,512]{2,1,0:T(8,128)(2,1)}), bf16[16,192,512]{2,1,0:T(8,128)(2,1)S(1)}, u32[]{:S(2)}, u32[]{:S(2)}) async-start(bf16[16,192,512]{2,1,0:T(8,128)(2,1)} %bitcast.22), calls=%async_computation.1 | async-start | bytes 6291456 | tf_op jit(solution)/shard_map/all_to_all | solution.py:179
  36.7 0.0 copy-done.5
  36.7 0.1 copy.12
  36.8 0.1 reduce.1
  36.9 0.0 copy-done.4
  36.9 0.1 convert_reduce_fusion
  37.0 0.1 select_reduce_fusion
  37.2 68.5 %all-to-all-done.1 = bf16[16,192,512]{2,1,0:T(8,128)(2,1)S(1)} async-done(((bf16[16,192,512]{2,1,0:T(8,128)(2,1)}), bf16[16,192,512]{2,1,0:T(8,128)(2,1)S(1)}, u32[]{:S(2)}, u32[]{:S(2)}) %all-to-all-start.1) | async-done | bytes 3145760 | tf_op jit(solution)/shard_map/all_to_all | solution.py:179
  105.7 9.2 %gather_fusion.1 = bf16[2048,512]{1,0:T(8,128)(2,1)} fusion(bf16[3072,512]{1,0:T(8,128)(2,1)S(1)} %bitcast.21, s32[2048]{0:T(1024)S(1)} %broadcast_clamp_fusion.1), kind=kCustom, calls=%fused_computation.1 | custom fusion | bytes 4202496 | tf_op jit(solution)/shard_map/gather | solution.py:194
  114.9 10.1 %project.1 = (bf16[2048,512]{1,0:T(8,128)(2,1)S(1)}, bf16[2048,512]{1,0:T(8,128)(2,1)S(1)}, bf16[2048,1024]{1,0:T(8,128)(2,1)}) custom-call(bf16[2048,512]{1,0:T(8,128)(2,1)} %gather_fusion.1, bf16[512,2048]{1,0:T(8,128)(2,1)} %w_ref.3), custom_call_target="tpu_custom_call" | custom-call | flops 4294967296 | bytes 12582912 | tf_op jit(solution)/shard_map/project/pallas_call | solution.py:52
  125.0 0.0 copy-start.1
  125.0 0.0 copy-start
  125.0 0.0 copy-start.3
  125.0 4.6 %slice.3 = bf16[1024,1024]{1,0:T(8,128)(2,1)} slice(bf16[2048,1024]{1,0:T(8,128)(2,1)} %get-tuple-element.9.before_ref.own_ref), slice={[1024:2048], [0:1024]} | slice | bytes 4194304 | tf_op jit(solution)/shard_map/slice | solution.py:201
  129.6 0.0 copy-done.1
  129.6 2.7 %collective-permute-start = (bf16[1024,1024]{1,0:T(8,128)(2,1)}, bf16[1024,1024]{1,0:T(8,128)(2,1)}, u32[]{:S(2)}, u32[]{:S(2)}) collective-permute-start(bf16[1024,1024]{1,0:T(8,128)(2,1)} %slice.3), channel_id=1, source_target_pairs={{0,1},{2,3},{4,5},{6,7},{8,9},{10,11},{12,13},{14,15},{16,17},{18,... | collective-permute-start | bytes 6291464 | tf_op jit(solution)/shard_map/ppermute | solution.py:19
  132.9 0.0 copy-done
  132.9 0.0 copy-done.3
  132.9 0.0 copy-start.2
  132.9 1.6 %copy-done.2 = bf16[2048,512]{1,0:T(8,128)(2,1)S(1)} copy-done((bf16[2048,512]{1,0:T(8,128)(2,1)S(1)}, bf16[2048,512]{1,0:T(8,128)(2,1)}, u32[]{:S(2)}) %copy-start.2) | copy-done | bytes 2097176
  134.5 11.4 %attend.2.rest_0_ = bf16[2048,512]{1,0:T(8,128)(2,1)} custom-call(s32[1]{0:T(128)S(6)} %sub.30.live_ref, bf16[2048,512]{1,0:T(8,128)(2,1)S(1)} %copy-done.2, bf16[2048,1024]{1,0:T(8,128)(2,1)} %get-tuple-element.9.before_ref.own_ref, bf16[2048,1024]{1,0:T(8,128)(2,1)} %get-tuple-element.9.before_ref.own_ref, ...), custom_call_target="tpu_custom_call" | custom-call | flops 3221225472 | bytes 8912896 | tf_op jit(solution)/shard_map/attend/pallas_call | solution.py:153
  145.9 0.0 collective-permute-done.before_ref
  145.9 11.5 %attend.3 = bf16[2048,512]{1,0:T(8,128)(2,1)} custom-call(s32[1]{0:T(128)S(6)} %sub.27.live_ref, bf16[2048,512]{1,0:T(8,128)(2,1)S(1)} %copy-done.2, bf16[1024,1024]{1,0:T(8,128)(2,1)} %collective-permute-done.before_ref, bf16[2048,1024]{1,0:T(8,128)(2,1)} %get-tuple-element.9.before_ref.own_ref, ...), custom_call_target="tpu_custom_call", output_to_operand_aliasing={{}: (7, {})} | custom-call | flops 3221225472 | bytes 8912896 | tf_op jit(solution)/shard_map/attend/pallas_call | solution.py:153
  (6 shorter events, 0.1 us)
Async XLA Ops:
  30.6 6.0 %copy-start.5 = (s32[1,1,16]{2,1,0:T(1,128)S(1)}, s32[1,1,16]{2,1,0:T(1,128)}, u32[]{:S(2)}) copy-start(s32[1,1,16]{2,1,0:T(1,128)} %param.9) | copy-start | bytes 196
  30.6 6.3 %copy-start.4 = (s32[1,1,2048]{2,1,0:T(1,128)S(1)}, s32[1,1,2048]{2,1,0:T(1,128)}, u32[]{:S(2)}) copy-start(s32[1,1,2048]{2,1,0:T(1,128)} %param.10) | copy-start | bytes 24580
  30.6 75.1 %all-to-all-start.1 = ((bf16[16,192,512]{2,1,0:T(8,128)(2,1)}), bf16[16,192,512]{2,1,0:T(8,128)(2,1)S(1)}, u32[]{:S(2)}, u32[]{:S(2)}) async-start(bf16[16,192,512]{2,1,0:T(8,128)(2,1)} %bitcast.22), calls=%async_computation.1 | async-start | bytes 6291456 | tf_op jit(solution)/shard_map/all_to_all | solution.py:179
  125.0 4.6 %copy-start.1 = (bf16[2048,512]{1,0:T(8,128)(2,1)}, bf16[2048,512]{1,0:T(8,128)(2,1)S(1)}, u32[]{:S(2)}) copy-start(bf16[2048,512]{1,0:T(8,128)(2,1)S(1)} %get-tuple-element.8.query_ref) | copy-start | bytes 6291460
  125.0 7.9 %copy-start = (bf16[2048,512]{1,0:T(8,128)(2,1)}, bf16[2048,512]{1,0:T(8,128)(2,1)S(1)}, u32[]{:S(2)}) copy-start(bf16[2048,512]{1,0:T(8,128)(2,1)S(1)} %get-tuple-element.10.gate_ref) | copy-start | bytes 6291460
  125.0 7.9 %copy-start.3 = (bf16[512,512]{1,0:T(8,128)(2,1)S(1)}, bf16[512,512]{1,0:T(8,128)(2,1)}, u32[]{:S(2)}) copy-start(bf16[512,512]{1,0:T(8,128)(2,1)} %w_ref.5) | copy-start | bytes 1572868
  129.6 16.4 %collective-permute-start = (bf16[1024,1024]{1,0:T(8,128)(2,1)}, bf16[1024,1024]{1,0:T(8,128)(2,1)}, u32[]{:S(2)}, u32[]{:S(2)}) collective-permute-start(bf16[1024,1024]{1,0:T(8,128)(2,1)} %slice.3), channel_id=1, source_target_pairs={{0,1},{2,3},{4,5},{6,7},{8,9},{10,11},{12,13},{14,15},{16,17},{18,... | collective-permute-start | bytes 6291464 | tf_op jit(solution)/shard_map/ppermute | solution.py:19
  132.9 1.6 %copy-start.2 = (bf16[2048,512]{1,0:T(8,128)(2,1)S(1)}, bf16[2048,512]{1,0:T(8,128)(2,1)}, u32[]{:S(2)}) copy-start(bf16[2048,512]{1,0:T(8,128)(2,1)} %copy-done.1) | copy-start | bytes 6291460

commit v2 on v1

--- a/solution.py
+++ b/solution.py
@@ -11,6 +11,7 @@
 WINDOW = 1024
 BLOCK = 256
 VMEM_LIMIT = 48 * 1024 * 1024
+LOOK_UP_LIMIT = 56 * 1024 * 1024
 
 
 def passed_along(value, axis, steps):
@@ -171,27 +172,209 @@
     )(*operands)
 
 
+def peer_offset(step, count):
+    if count % 2:
+        return step + 1
+    away = (step + 1) // 2
+    return count // 2 + away * (1 - 2 * (step % 2))
+
+
+def look_up_kernel(
+    ids_ref,
+    keys_ref,
+    rank_ref,
+    table_ref,
+    out_ref,
+    ids_held,
+    ids_scalar,
+    staged,
+    table_wide,
+    rank_wide,
+    rows_wide,
+    sent,
+    received,
+    stage_sems,
+    scalar_sem,
+    ids_send_sems,
+    ids_recv_sems,
+    send_sems,
+    recv_sems,
+):
+    shards, capacity, width = sent.shape
+    tokens = out_ref.shape[0]
+    parts, part_rows = staged.shape[0], staged.shape[1]
+    me = lax.axis_index("table")
+    mesh_ids = pl.DeviceIdType.MESH
+
+    def stage(part):
+        return pltpu.make_async_copy(
+            table_ref.at[pl.ds(pl.multiple_of(part * part_rows, part_rows), part_rows)],
+            staged.at[part],
+            stage_sems.at[part],
+        )
+
+    for part in range(parts):
+        stage(part).start()
+
+    barrier = pltpu.get_barrier_semaphore()
+
+    @pl.loop(1, shards)
+    def _(offset):
+        peer = lax.rem(me + offset, shards)
+        pl.semaphore_signal(barrier, inc=1, device_id={"table": peer}, device_id_type=mesh_ids)
+
+    pl.semaphore_wait(barrier, shards - 1)
+
+    def send_ids(offset):
+        peer = lax.rem(me + offset, shards)
+        return pltpu.make_async_remote_copy(
+            src_ref=ids_ref.at[peer],
+            dst_ref=ids_held.at[me],
+            send_sem=ids_send_sems.at[offset],
+            recv_sem=ids_recv_sems.at[me],
+            device_id={"table": peer},
+            device_id_type=mesh_ids,
+        )
+
+    def take_ids(source):
+        return pltpu.make_async_remote_copy(
+            src_ref=ids_ref.at[source],
+            dst_ref=ids_held.at[source],
+            send_sem=ids_send_sems.at[0],
+            recv_sem=ids_recv_sems.at[source],
+            device_id={"table": source},
+            device_id_type=mesh_ids,
+        )
+
+    @pl.loop(1, shards)
+    def _(offset):
+        send_ids(offset).start()
+
+    ids_held[me] = ids_ref[me]
+    rank_wide[...] = jnp.broadcast_to(rank_ref[...], rank_wide.shape)
+
+    for part in range(parts):
+        stage(part).wait()
+
+        @pl.loop(0, part_rows, step=64)
+        def _(first):
+            first = pl.multiple_of(first, 64)
+            target = pl.multiple_of(part * part_rows + first, 64)
+            table_wide[pl.ds(target, 64)] = staged[part, pl.ds(first, 64)].astype(jnp.float32)
+
+    @pl.loop(1, shards)
+    def _(offset):
+        take_ids(lax.rem(me + offset, shards)).wait_recv()
+
+    to_scalar = pltpu.make_async_copy(ids_held, ids_scalar, scalar_sem)
+    to_scalar.start()
+    to_scalar.wait()
+
+    def gather(peer):
+        @pl.loop(0, capacity, step=16)
+        def _(first):
+            for i in range(16):
+                row = ids_scalar[peer, 0, first + i]
+                rows_wide[pl.ds(first + i, 1)] = table_wide[pl.ds(row, 1)]
+
+        return rows_wide[...].astype(jnp.bfloat16)
+
+    def send_rows(offset):
+        peer = lax.rem(me + offset, shards)
+        return pltpu.make_async_remote_copy(
+            src_ref=sent.at[offset],
+            dst_ref=received.at[me],
+            send_sem=send_sems.at[offset],
+            recv_sem=recv_sems.at[me],
+            device_id={"table": peer},
+            device_id_type=mesh_ids,
+        )
+
+    def take_rows(source):
+        return pltpu.make_async_remote_copy(
+            src_ref=sent.at[0],
+            dst_ref=received.at[source],
+            send_sem=send_sems.at[0],
+            recv_sem=recv_sems.at[source],
+            device_id={"table": source},
+            device_id_type=mesh_ids,
+        )
+
+    @pl.loop(0, shards - 1)
+    def _(step):
+        offset = peer_offset(step, shards)
+        sent[offset] = gather(lax.rem(me + offset, shards))
+        send_rows(offset).start()
+
+    received[me] = gather(me)
+
+    def place(source, add):
+        keys = keys_ref[source]
+
+        @pl.loop(0, tokens, step=256)
+        def _(first):
+            at = pl.ds(pl.multiple_of(first, 256), 256)
+            chosen = jnp.where(rank_wide[at] == keys, 1.0, 0.0).astype(jnp.bfloat16)
+            found = jnp.dot(chosen, received[source], preferred_element_type=jnp.float32)
+            found = found.astype(jnp.bfloat16)
+            out_ref[at] = out_ref[at] + found if add else found
+
+    place(me, False)
+
+    @pl.loop(0, shards - 1)
+    def _(step):
+        source = lax.rem(me + shards - peer_offset(step, shards), shards)
+        take_rows(source).wait_recv()
+        place(source, True)
+
+    @pl.loop(1, shards)
+    def _(offset):
+        send_ids(offset).wait_send()
+        send_rows(offset).wait_send()
+
+
 def look_up(embed_table, lookup_ids, counts, event_order):
     shards = lax.axis_size("table")
     capacity = lookup_ids.shape[3]
-    width = embed_table.shape[1]
-    requests = lookup_ids[0, 0]
-    fetched = lax.all_to_all(
-        embed_table[lax.all_to_all(requests, "table", split_axis=0, concat_axis=0, tiled=True)],
-        "table",
-        split_axis=0,
-        concat_axis=0,
-        tiled=True,
-    )
+    tokens = event_order.shape[2]
+    rows, width = embed_table.shape
+    parts = 8 if rows % 1024 == 0 else 1
     live_counts = counts[0, 0]
-    totals = jnp.cumsum(live_counts)
-    starts = totals - live_counts
-    event_rank = event_order[0, 0]
-    owner_shard = jnp.sum((event_rank[:, None] >= totals[None, :]).astype(jnp.int32), axis=1)
-    chosen = owner_shard[:, None] == jnp.arange(shards, dtype=jnp.int32)[None, :]
-    slot_start = jnp.sum(jnp.where(chosen, starts[None, :], 0), axis=1)
-    slot_index = owner_shard * capacity + event_rank - slot_start
-    return fetched.reshape(shards * capacity, width)[slot_index]
+    starts = jnp.cumsum(live_counts) - live_counts
+    slots = jnp.arange(capacity, dtype=jnp.int32)
+    keys = jnp.where(slots < live_counts[:, None], starts[:, None] + slots, -1)
+    vmem = pl.BlockSpec(memory_space=pltpu.VMEM)
+    return pl.pallas_call(
+        look_up_kernel,
+        in_specs=[vmem, vmem, vmem, pl.BlockSpec(memory_space=pl.ANY)],
+        out_specs=vmem,
+        out_shape=jax.ShapeDtypeStruct((tokens, width), jnp.bfloat16),
+        scratch_shapes=[
+            pltpu.VMEM((shards, 1, capacity), jnp.int32),
+            pltpu.SMEM((shards, 1, capacity), jnp.int32),
+            pltpu.VMEM((parts, rows // parts, width), jnp.bfloat16),
+            pltpu.VMEM((rows, width), jnp.float32),
+            pltpu.VMEM((tokens, capacity), jnp.int32),
+            pltpu.VMEM((capacity, width), jnp.float32),
+            pltpu.VMEM((shards, capacity, width), jnp.bfloat16),
+            pltpu.VMEM((shards, capacity, width), jnp.bfloat16),
+            pltpu.SemaphoreType.DMA((parts,)),
+            pltpu.SemaphoreType.DMA,
+            pltpu.SemaphoreType.DMA((shards,)),
+            pltpu.SemaphoreType.DMA((shards,)),
+            pltpu.SemaphoreType.DMA((shards,)),
+            pltpu.SemaphoreType.DMA((shards,)),
+        ],
+        compiler_params=pltpu.CompilerParams(
+            collective_id=0, has_side_effects=True, vmem_limit_bytes=LOOK_UP_LIMIT
+        ),
+        cost_estimate=pl.CostEstimate(
+            flops=2 * tokens * shards * capacity * width,
+            bytes_accessed=2 * rows * width + 4 * shards * capacity * width,
+            transcendentals=0,
+        ),
+        name="look_up",
+    )(lookup_ids[0, 0][:, None, :], keys[:, None, :], event_order[0, 0][:, None], embed_table)
 
 
 def local(embed_table, lookup_ids, counts, event_order, hist_len, w_uvqk, w_out):

time: 158 us -> 146 us (0.924)
  Pallas kernels: 33 us -> 130 us
  waiting for transfers between devices: 68.5 us -> 0.01 us
  local copies, waits for them, and re-layouts: 34 us -> 10.3 us
  blocking collectives: 12 us -> 0 us
  starting transfers between devices: 8.71 us -> 2.76 us
  other arithmetic: 0.44 us -> 2.17 us
    pallas_call x0 -> x1, Pallas kernels: none -> 97.1 us  [look_up(): pl.pallas_call(look_up_kernel, in_specs=[vmem, vmem, vmem, pl.BlockSpec(m...]
    all_to_all x1 -> x0, waiting for transfers between devices: 68.5 us -> none  [look_up(): lax.all_to_all(embed_table[lax.all_to_all(requests, 'table', split_axis=0...]
    gather x2 -> x0, local copies, waits for them, and re-layouts: 26.9 us -> none  [the longest x1 17.8 us: look_up(): embed_table[lax.all_to_all(requests, 'table', split_axis=0, concat_axis=0...]
    all_to_all x1 -> x0, blocking collectives: 12 us -> none  [look_up(): lax.all_to_all(requests, 'table', split_axis=0, concat_axis=0, tiled=True)]
    all_to_all x1 -> x0, starting transfers between devices: 6.03 us -> none  [look_up(): lax.all_to_all(embed_table[lax.all_to_all(requests, 'table', split_axis=0...]
    another operation x1 -> x3, local copies, waits for them, and re-layouts: 0.08 us -> 4.09 us  [the longest x1 2.04 us: look_up(): event_order[0, 0][:, None]]
  transfers between devices with their start and end apart: 2 -> 1, of which waited for: 1 -> 0; matrix products, arithmetic and copies ran while one was open for 0% -> 0% of each run, Pallas kernels for 7% -> 8%
where the time goes in v2:
time: 146 us
  Pallas kernels  130 us (89%)
  local copies, waits for them, and re-layouts  10.3 us (7%)
  starting transfers between devices  2.76 us (2%)
  other arithmetic  2.17 us (1%)
    pallas_call x1, Pallas kernels, look_up(): pl.pallas_call(look_up_kernel, in_specs=[vmem, vmem, vmem, pl.BlockSpec(m...  97.1 us
    pallas_call x2, Pallas kernels, attend(): pl.pallas_call(attend_kernel, grid=(per_part,), in_specs=in_specs, out_sp...  23 us
    pallas_call x1, Pallas kernels, project(): pl.pallas_call(functools.partial(project_kernel, query_scale), grid=(toke...  10.1 us
    slice x1, local copies, waits for them, and re-layouts, local(): before = passed_along(keyvals[tokens - WINDOW:], 'seq', 1)  4.6 us
  transfers between devices with their start and end apart: 1, of which 0 were waited for; matrix products, arithmetic and copies ran while one was open for 0% of the time, Pallas kernels for 8%

profile of v2, /device:TPU:16, one launch (start us, length us, event | category | flops | bytes accessed | tf_op | source)
XLA Modules:
  0.0 146.0 jit_solution(627291083912847846)
XLA Ops:
  0.0 1.3 broadcast_in_dim_squeeze.7.ids_ref
  1.3 0.7 copy.10
  2.1 0.1 reduce
  2.2 0.7 bitcast_subtract_fusion
  2.9 2.0 %copy.11.rank_ref = s32[2048,1]{1,0:T(8,128)} copy(s32[2048,1]{0,1:T(1,128)} %bitcast.8) | data formatting | bytes 16384 | tf_op jit(solution)/shard_map/broadcast_in_dim;squeeze | solution.py:377
  4.9 1.4 compare_select_fusion.keys_ref
  6.3 97.1 %look_up.1.events_ref = bf16[2048,512]{1,0:T(8,128)(2,1)} custom-call(s32[16,1,192]{2,1,0:T(1,128)} %broadcast_in_dim_squeeze.7.ids_ref, s32[16,1,192]{2,1,0:T(1,128)} %compare_select_fusion.keys_ref, s32[2048,1]{1,0:T(8,128)} %copy.11.rank_ref, bf16[8192,512]{1,0:T(8,128)(2,1)} %table_ref.1), custom_call_target="tpu_custom_call" | custom-call | flops 6442450944 | bytes 14680064 | tf_op jit(solution)/shard_map/look_up/pallas_call | solution.py:347
  103.3 10.1 %project.1 = (bf16[2048,512]{1,0:T(8,128)(2,1)S(1)}, bf16[2048,512]{1,0:T(8,128)(2,1)S(1)}, bf16[2048,1024]{1,0:T(8,128)(2,1)}) custom-call(bf16[2048,512]{1,0:T(8,128)(2,1)} %look_up.1.events_ref, bf16[512,2048]{1,0:T(8,128)(2,1)} %w_ref.3), custom_call_target="tpu_custom_call" | custom-call | flops 4294967296 | bytes 12582912 | tf_op jit(solution)/shard_map/project/pallas_call | solution.py:53
  113.4 0.0 copy-start.1
  113.4 0.0 copy-start
  113.4 0.0 copy-start.3
  113.4 4.6 %slice.3 = bf16[1024,1024]{1,0:T(8,128)(2,1)} slice(bf16[2048,1024]{1,0:T(8,128)(2,1)} %get-tuple-element.9.before_ref.own_ref), slice={[1024:2048], [0:1024]} | slice | bytes 4194304 | tf_op jit(solution)/shard_map/slice | solution.py:384
  118.0 0.0 copy-done.1
  118.0 2.8 %collective-permute-start = (bf16[1024,1024]{1,0:T(8,128)(2,1)}, bf16[1024,1024]{1,0:T(8,128)(2,1)}, u32[]{:S(2)}, u32[]{:S(2)}) collective-permute-start(bf16[1024,1024]{1,0:T(8,128)(2,1)} %slice.3), channel_id=1, source_target_pairs={{0,1},{2,3},{4,5},{6,7},{8,9},{10,11},{12,13},{14,15},{16,17},{18,... | collective-permute-start | bytes 6291464 | tf_op jit(solution)/shard_map/ppermute | solution.py:20
  121.5 0.0 copy-done
  121.5 0.0 copy-done.3
  121.5 0.0 copy-start.2
  121.5 1.6 %copy-done.2 = bf16[2048,512]{1,0:T(8,128)(2,1)S(1)} copy-done((bf16[2048,512]{1,0:T(8,128)(2,1)S(1)}, bf16[2048,512]{1,0:T(8,128)(2,1)}, u32[]{:S(2)}) %copy-start.2) | copy-done | bytes 2097176
  123.1 11.4 %attend.2.rest_0_ = bf16[2048,512]{1,0:T(8,128)(2,1)} custom-call(s32[1]{0:T(128)S(6)} %sub.19.live_ref, bf16[2048,512]{1,0:T(8,128)(2,1)S(1)} %copy-done.2, bf16[2048,1024]{1,0:T(8,128)(2,1)} %get-tuple-element.9.before_ref.own_ref, bf16[2048,1024]{1,0:T(8,128)(2,1)} %get-tuple-element.9.before_ref.own_ref, ...), custom_call_target="tpu_custom_call" | custom-call | flops 3221225472 | bytes 8912896 | tf_op jit(solution)/shard_map/attend/pallas_call | solution.py:154
  134.5 0.0 collective-permute-done.before_ref
  134.5 11.5 %attend.3 = bf16[2048,512]{1,0:T(8,128)(2,1)} custom-call(s32[1]{0:T(128)S(6)} %sub.17.live_ref, bf16[2048,512]{1,0:T(8,128)(2,1)S(1)} %copy-done.2, bf16[1024,1024]{1,0:T(8,128)(2,1)} %collective-permute-done.before_ref, bf16[2048,1024]{1,0:T(8,128)(2,1)} %get-tuple-element.9.before_ref.own_ref, ...), custom_call_target="tpu_custom_call", output_to_operand_aliasing={{}: (7, {})} | custom-call | flops 3221225472 | bytes 8912896 | tf_op jit(solution)/shard_map/attend/pallas_call | solution.py:154
  (1 shorter events, 0.0 us)
Async XLA Ops:
  113.4 4.6 %copy-start.1 = (bf16[2048,512]{1,0:T(8,128)(2,1)}, bf16[2048,512]{1,0:T(8,128)(2,1)S(1)}, u32[]{:S(2)}) copy-start(bf16[2048,512]{1,0:T(8,128)(2,1)S(1)} %get-tuple-element.8.query_ref) | copy-start | bytes 6291460
  113.4 8.0 %copy-start = (bf16[2048,512]{1,0:T(8,128)(2,1)}, bf16[2048,512]{1,0:T(8,128)(2,1)S(1)}, u32[]{:S(2)}) copy-start(bf16[2048,512]{1,0:T(8,128)(2,1)S(1)} %get-tuple-element.10.gate_ref) | copy-start | bytes 6291460
  113.4 8.0 %copy-start.3 = (bf16[512,512]{1,0:T(8,128)(2,1)S(1)}, bf16[512,512]{1,0:T(8,128)(2,1)}, u32[]{:S(2)}) copy-start(bf16[512,512]{1,0:T(8,128)(2,1)} %w_ref.5) | copy-start | bytes 1572868
  118.0 16.5 %collective-permute-start = (bf16[1024,1024]{1,0:T(8,128)(2,1)}, bf16[1024,1024]{1,0:T(8,128)(2,1)}, u32[]{:S(2)}, u32[]{:S(2)}) collective-permute-start(bf16[1024,1024]{1,0:T(8,128)(2,1)} %slice.3), channel_id=1, source_target_pairs={{0,1},{2,3},{4,5},{6,7},{8,9},{10,11},{12,13},{14,15},{16,17},{18,... | collective-permute-start | bytes 6291464 | tf_op jit(solution)/shard_map/ppermute | solution.py:20
  121.5 1.6 %copy-start.2 = (bf16[2048,512]{1,0:T(8,128)(2,1)S(1)}, bf16[2048,512]{1,0:T(8,128)(2,1)}, u32[]{:S(2)}) copy-start(bf16[2048,512]{1,0:T(8,128)(2,1)} %copy-done.1) | copy-start | bytes 6291460

commit v3 on v2

--- a/solution.py
+++ b/solution.py
@@ -10,6 +10,7 @@
 HEADS = 4
 WINDOW = 1024
 BLOCK = 256
+LANES = 128
 VMEM_LIMIT = 48 * 1024 * 1024
 LOOK_UP_LIMIT = 56 * 1024 * 1024
 
@@ -31,7 +32,7 @@
     return half + half * jnp.tanh(half)
 
 
-def project_kernel(query_scale, events_ref, w_ref, gate_ref, query_ref, keyval_ref):
+def project_kernel(query_scale, events_ref, w_ref, gate_ref, query_ref, keyval_ref, last_ref):
     width = events_ref.shape[1]
     normed = normalize(events_ref[...].astype(jnp.float32)).astype(jnp.bfloat16)
 
@@ -44,10 +45,15 @@
     keyval_ref[:, :width] = columns(2 * width, width).astype(keyval_ref.dtype)
     keyval_ref[:, width:] = columns(3 * width, width).astype(keyval_ref.dtype)
 
+    @pl.when(pl.program_id(0) >= pl.num_programs(0) - WINDOW // events_ref.shape[0])
+    def _():
+        last_ref[...] = keyval_ref[...]
+
 
 def project(events, w_uvqk):
     tokens, width = events.shape
     rows = 512
+    skipped = (tokens - WINDOW) // rows
     query_scale = 0.5 * (width // HEADS) ** (-0.5)
     kind = jnp.bfloat16
     return pl.pallas_call(
@@ -61,11 +67,13 @@
             pl.BlockSpec((rows, width), lambda i: (i, 0)),
             pl.BlockSpec((rows, width), lambda i: (i, 0)),
             pl.BlockSpec((rows, 2 * width), lambda i: (i, 0)),
+            pl.BlockSpec((rows, 2 * width), lambda i: (jnp.maximum(i - skipped, 0), 0)),
         ],
         out_shape=[
             jax.ShapeDtypeStruct((tokens, width), kind),
             jax.ShapeDtypeStruct((tokens, width), kind),
             jax.ShapeDtypeStruct((tokens, 2 * width), kind),
+            jax.ShapeDtypeStruct((WINDOW, 2 * width), kind),
         ],
         compiler_params=pltpu.CompilerParams(vmem_limit_bytes=VMEM_LIMIT),
         cost_estimate=pl.CostEstimate(
@@ -175,16 +183,21 @@
 def peer_offset(step, count):
     if count % 2:
         return step + 1
-    away = (step + 1) // 2
-    return count // 2 + away * (1 - 2 * (step % 2))
+    turn = step // 2
+    away = (turn + 1) // 2
+    far = count // 2 + away * (1 - 2 * (turn % 2))
+    near = lax.rem(count - 1 - turn // 2 + (turn % 2) * (turn + 1), count)
+    return jnp.where(step % 2 == 0, far, near)
 
 
 def look_up_kernel(
-    ids_ref,
-    keys_ref,
-    rank_ref,
+    lookup_ref,
+    counts_ref,
+    order_ref,
     table_ref,
     out_ref,
+    ids_ref,
+    starts,
     ids_held,
     ids_scalar,
     staged,
@@ -216,6 +229,9 @@
     for part in range(parts):
         stage(part).start()
 
+    for shard in range(shards):
+        ids_ref[shard] = lookup_ref[0, 0, shard : shard + 1]
+
     barrier = pltpu.get_barrier_semaphore()
 
     @pl.loop(1, shards)
@@ -251,7 +267,17 @@
         send_ids(offset).start()
 
     ids_held[me] = ids_ref[me]
-    rank_wide[...] = jnp.broadcast_to(rank_ref[...], rank_wide.shape)
+    start = jnp.int32(0)
+    for shard in range(shards):
+        starts[shard] = start
+        start = start + counts_ref[0, 0, shard]
+
+    for first in range(0, tokens, LANES):
+        ranks = order_ref[0, :, first : first + LANES]
+        ranks = jnp.transpose(jnp.broadcast_to(ranks, (LANES, LANES)))
+        for column in range(0, capacity, LANES):
+            count = min(LANES, capacity - column)
+            rank_wide[first : first + LANES, column : column + count] = ranks[:, :count]
 
     for part in range(parts):
         stage(part).wait()
@@ -309,7 +335,8 @@
     received[me] = gather(me)
 
     def place(source, add):
-        keys = keys_ref[source]
+        slot = lax.broadcasted_iota(jnp.int32, (1, capacity), 1)
+        keys = jnp.where(slot < counts_ref[0, 0, source], starts[source] + slot, -1)
 
         @pl.loop(0, tokens, step=256)
         def _(first):
@@ -339,17 +366,20 @@
     tokens = event_order.shape[2]
     rows, width = embed_table.shape
     parts = 8 if rows % 1024 == 0 else 1
-    live_counts = counts[0, 0]
-    starts = jnp.cumsum(live_counts) - live_counts
-    slots = jnp.arange(capacity, dtype=jnp.int32)
-    keys = jnp.where(slots < live_counts[:, None], starts[:, None] + slots, -1)
     vmem = pl.BlockSpec(memory_space=pltpu.VMEM)
     return pl.pallas_call(
         look_up_kernel,
-        in_specs=[vmem, vmem, vmem, pl.BlockSpec(memory_space=pl.ANY)],
+        in_specs=[
+            vmem,
+            pl.BlockSpec(memory_space=pltpu.SMEM),
+            vmem,
+            pl.BlockSpec(memory_space=pl.ANY),
+        ],
         out_specs=vmem,
         out_shape=jax.ShapeDtypeStruct((tokens, width), jnp.bfloat16),
         scratch_shapes=[
+            pltpu.VMEM((shards, 1, capacity), jnp.int32),
+            pltpu.SMEM((shards,), jnp.int32),
             pltpu.VMEM((shards, 1, capacity), jnp.int32),
             pltpu.SMEM((shards, 1, capacity), jnp.int32),
             pltpu.VMEM((parts, rows // parts, width), jnp.bfloat16),
@@ -374,14 +404,14 @@
             transcendentals=0,
         ),
         name="look_up",
-    )(lookup_ids[0, 0][:, None, :], keys[:, None, :], event_order[0, 0][:, None], embed_table)
+    )(lookup_ids, counts, event_order, embed_table)
 
 
 def local(embed_table, lookup_ids, counts, event_order, hist_len, w_uvqk, w_out):
     events = look_up(embed_table, lookup_ids, counts, event_order)
     tokens = events.shape[0]
-    gate, queries, keyvals = project(events, w_uvqk)
-    before = passed_along(keyvals[tokens - WINDOW :], "seq", 1)
+    gate, queries, keyvals, last = project(events, w_uvqk)
+    before = passed_along(last, "seq", 1)
     live = hist_len - lax.axis_index("seq") * tokens
     out = None
     for part in reversed(range(tokens // WINDOW)):

time: 146 us -> 127 us (0.87); the launches traced: 146 us -> 126 us
  Pallas kernels: 130 us -> 119 us
  local copies, waits for them, and re-layouts: 10.3 us -> 2.91 us
  other arithmetic: 2.17 us -> 0 us
    pallas_call x1, Pallas kernels: 97.1 us -> 85.5 us  [look_up(): pl.pallas_call(look_up_kernel, in_specs=[vmem, pl.BlockSpec(memory_space=...]
    slice x1 -> x0, local copies, waits for them, and re-layouts: 4.6 us -> none  [local(): before = passed_along(keyvals[tokens - WINDOW:], 'seq', 1)]
    another operation x3 -> x0, local copies, waits for them, and re-layouts: 4.09 us -> none  [the longest x1 2.04 us: look_up(): event_order[0, 0][:, None]]
  transfers between devices with their start and end apart: 1 -> 1, of which waited for: 0 -> 0; matrix products, arithmetic and copies ran while one was open for 0% -> 0% of each run, Pallas kernels for 8% -> 9%
where the time goes in v3:
time: 127 us; the launch traced here: 126 us
  Pallas kernels  119 us (94%)
  local copies, waits for them, and re-layouts  2.91 us (2%)
  starting transfers between devices  2.86 us (2%)
    pallas_call x1, Pallas kernels, look_up(): pl.pallas_call(look_up_kernel, in_specs=[vmem, pl.BlockSpec(memory_space=...  85.5 us
    pallas_call x2, Pallas kernels, attend(): pl.pallas_call(attend_kernel, grid=(per_part,), in_specs=in_specs, out_sp...  23 us
    pallas_call x1, Pallas kernels, project(): pl.pallas_call(functools.partial(project_kernel, query_scale), grid=(toke...  10.6 us
    unnamed x8, local copies, waits for them, and re-layouts  2.91 us
    ppermute x1, starting transfers between devices, passed_along(): lax.ppermute(value, axis, [(source, source + steps) for source in range(i...  2.86 us
  transfers between devices with their start and end apart: 1, of which 0 were waited for; matrix products, arithmetic and copies ran while one was open for 0% of the time, Pallas kernels for 9%

profile of v3, /device:TPU:16, one launch (start us, length us, event | category | flops | bytes accessed | tf_op | source)
XLA Modules:
  0.0 125.6 jit_solution(4647544027123481422)
XLA Ops:
  0.0 85.5 %look_up.1.events_ref = bf16[2048,512]{1,0:T(8,128)(2,1)} custom-call(s32[1,1,16,192]{3,2,1,0:T(8,128)} %lookup_ref.1, s32[1,1,16]{2,1,0:T(1,128)} %counts_ref.1, s32[1,1,2048]{2,1,0:T(1,128)} %order_ref.1, bf16[8192,512]{1,0:T(8,128)(2,1)} %table_ref.1), custom_call_target="tpu_custom_call" | custom-call | flops 6442450944 | bytes 14680064 | tf_op jit(solution)/shard_map/look_up/pallas_call | solution.py:370
  85.5 0.0 copy-start.3
  85.5 10.6 %project.1 = (bf16[2048,512]{1,0:T(8,128)(2,1)S(1)}, bf16[2048,512]{1,0:T(8,128)(2,1)S(1)}, bf16[2048,1024]{1,0:T(8,128)(2,1)}, bf16[1024,1024]{1,0:T(8,128)(2,1)}) custom-call(bf16[2048,512]{1,0:T(8,128)(2,1)} %look_up.1.events_ref, bf16[512,2048]{1,0:T(8,128)(2,1)} %w_ref.3), custom_call_target="tpu_custom_call" | custom-call | flops 4294967296 | bytes 12582912 | tf_op jit(solution)/shard_map/project/pallas_call | solution.py:59
  96.1 0.0 copy-start.1
  96.1 1.3 %copy-done.1 = bf16[2048,512]{1,0:T(8,128)(2,1)} copy-done((bf16[2048,512]{1,0:T(8,128)(2,1)}, bf16[2048,512]{1,0:T(8,128)(2,1)S(1)}, u32[]{:S(2)}) %copy-start.1) | copy-done | bytes 2097176
  97.5 0.0 copy-start
  97.5 2.9 %collective-permute-start = (bf16[1024,1024]{1,0:T(8,128)(2,1)}, bf16[1024,1024]{1,0:T(8,128)(2,1)}, u32[]{:S(2)}, u32[]{:S(2)}) collective-permute-start(bf16[1024,1024]{1,0:T(8,128)(2,1)} %get-tuple-element.10), channel_id=1, source_target_pairs={{0,1},{2,3},{4,5},{6,7},{8,9},{10,11},{12,13},{14,15},{16,17},{18,... | collective-permute-start | bytes 6291464 | tf_op jit(solution)/shard_map/ppermute | solution.py:21
  101.0 0.0 copy-done.3
  101.0 0.0 copy-start.2
  101.0 1.6 %copy-done.2 = bf16[2048,512]{1,0:T(8,128)(2,1)S(1)} copy-done((bf16[2048,512]{1,0:T(8,128)(2,1)S(1)}, bf16[2048,512]{1,0:T(8,128)(2,1)}, u32[]{:S(2)}) %copy-start.2) | copy-done | bytes 2097176
  102.6 11.4 %attend.2.rest_0_ = bf16[2048,512]{1,0:T(8,128)(2,1)} custom-call(s32[1]{0:T(128)S(6)} %sub.11.live_ref, bf16[2048,512]{1,0:T(8,128)(2,1)S(1)} %copy-done.2, bf16[2048,1024]{1,0:T(8,128)(2,1)} %get-tuple-element.11.before_ref.own_ref, bf16[2048,1024]{1,0:T(8,128)(2,1)} %get-tuple-element.11.before_ref.own_ref, ...), custom_call_target="tpu_custom_call" | custom-call | flops 3221225472 | bytes 8912896 | tf_op jit(solution)/shard_map/attend/pallas_call | solution.py:162
  114.0 0.0 copy-done
  114.0 0.0 collective-permute-done.before_ref
  114.0 11.5 %attend.3 = bf16[2048,512]{1,0:T(8,128)(2,1)} custom-call(s32[1]{0:T(128)S(6)} %sub.10.live_ref, bf16[2048,512]{1,0:T(8,128)(2,1)S(1)} %copy-done.2, bf16[1024,1024]{1,0:T(8,128)(2,1)} %collective-permute-done.before_ref, bf16[2048,1024]{1,0:T(8,128)(2,1)} %get-tuple-element.11.before_ref.own_ref, ...), custom_call_target="tpu_custom_call", output_to_operand_aliasing={{}: (7, {})} | custom-call | flops 3221225472 | bytes 8912896 | tf_op jit(solution)/shard_map/attend/pallas_call | solution.py:162
Async XLA Ops:
  85.5 15.5 %copy-start.3 = (bf16[512,512]{1,0:T(8,128)(2,1)S(1)}, bf16[512,512]{1,0:T(8,128)(2,1)}, u32[]{:S(2)}) copy-start(bf16[512,512]{1,0:T(8,128)(2,1)} %w_ref.5) | copy-start | bytes 1572868
  96.1 1.3 %copy-start.1 = (bf16[2048,512]{1,0:T(8,128)(2,1)}, bf16[2048,512]{1,0:T(8,128)(2,1)S(1)}, u32[]{:S(2)}) copy-start(bf16[2048,512]{1,0:T(8,128)(2,1)S(1)} %get-tuple-element.9.query_ref) | copy-start | bytes 6291460
  97.5 16.5 %copy-start = (bf16[2048,512]{1,0:T(8,128)(2,1)}, bf16[2048,512]{1,0:T(8,128)(2,1)S(1)}, u32[]{:S(2)}) copy-start(bf16[2048,512]{1,0:T(8,128)(2,1)S(1)} %get-tuple-element.12.gate_ref) | copy-start | bytes 6291460
  97.5 16.5 %collective-permute-start = (bf16[1024,1024]{1,0:T(8,128)(2,1)}, bf16[1024,1024]{1,0:T(8,128)(2,1)}, u32[]{:S(2)}, u32[]{:S(2)}) collective-permute-start(bf16[1024,1024]{1,0:T(8,128)(2,1)} %get-tuple-element.10), channel_id=1, source_target_pairs={{0,1},{2,3},{4,5},{6,7},{8,9},{10,11},{12,13},{14,15},{16,17},{18,... | collective-permute-start | bytes 6291464 | tf_op jit(solution)/shard_map/ppermute | solution.py:21
  101.0 1.6 %copy-start.2 = (bf16[2048,512]{1,0:T(8,128)(2,1)S(1)}, bf16[2048,512]{1,0:T(8,128)(2,1)}, u32[]{:S(2)}) copy-start(bf16[2048,512]{1,0:T(8,128)(2,1)} %copy-done.1) | copy-start | bytes 6291460

commit v4 on v3

v4 whole, which is shorter than its diff:
```python
import jax
import jax.numpy as jnp
from jax import lax
from jax.experimental import pallas as pl
from jax.experimental.pallas import tpu as pltpu
from jax.sharding import PartitionSpec as P

HEADS = 4
WINDOW = 1024
BLOCK = 256
LANES = 128
VMEM_LIMIT = 60 * 1024 * 1024


def normalize(values):
    average = jnp.mean(values, axis=-1, keepdims=True)
    centered = values - average
    spread = jnp.mean(centered * centered, axis=-1, keepdims=True)
    return centered * lax.rsqrt(spread + 1e-05)


def silu_of_double(half):
    return half + half * jnp.tanh(half)


def scores_of(queries, keys):
    return lax.dot_general(
        queries, keys, (((1,), (1,)), ((), ())), preferred_element_type=jnp.float32
    )


def dot32(left, right):
    return jnp.dot(left, right, preferred_element_type=jnp.float32)


def peer_offset(step, count):
    if count % 2:
        return step + 1
    turn = step // 2
    away = (turn + 1) // 2
    far = count // 2 + away * (1 - 2 * (turn % 2))
    near = lax.rem(count - 1 - turn // 2 + (turn % 2) * (turn + 1), count)
    return jnp.where(step % 2 == 0, far, near)


def layer_kernel(
    lookup_ref,
    counts_ref,
    order_ref,
    live_ref,
    table_ref,
    w_in_ref,
    w_out_ref,
    out_ref,
    ids_ref,
    starts,
    ids_held,
    ids_scalar,
    staged,
    table_wide,
    rank_wide,
    rows_wide,
    sent,
    received,
    stage_sems,
    scalar_sem,
    ids_send_sems,
    ids_recv_sems,
    send_sems,
    recv_sems,
    w_in,
    w_out,
    weight_sems,
    events,
    gate,
    queries,
    context,
    heads_out,
    result,
    result_sems,
    halo_send_sem,
    halo_recv_sem,
):
    shards, capacity, width = sent.shape
    tokens = events.shape[0]
    slots, part_rows = staged.shape[0], staged.shape[1]
    parts = table_ref.shape[0] // part_rows
    me = lax.axis_index("table")
    piece, pieces = lax.axis_index("seq"), lax.axis_size("seq")
    mesh_ids = pl.DeviceIdType.MESH

    def stage(part):
        return pltpu.make_async_copy(
            table_ref.at[pl.ds(pl.multiple_of(part * part_rows, part_rows), part_rows)],
            staged.at[part % slots],
            stage_sems.at[part % slots],
        )

    for part in range(slots):
        stage(part).start()
    load_in = pltpu.make_async_copy(w_in_ref, w_in, weight_sems.at[0])
    load_out = pltpu.make_async_copy(w_out_ref, w_out, weight_sems.at[1])
    load_in.start()
    load_out.start()

    for shard in range(shards):
        ids_ref[shard] = lookup_ref[0, 0, shard : shard + 1]

    barrier = pltpu.get_barrier_semaphore()

    @pl.loop(1, shards)
    def _(offset):
        peer = lax.rem(me + offset, shards)
        pl.semaphore_signal(barrier, inc=1, device_id={"table": peer}, device_id_type=mesh_ids)

    @pl.when(piece > 0)
    def _():
        pl.semaphore_signal(barrier, inc=1, device_id={"seq": piece - 1}, device_id_type=mesh_ids)

    @pl.when(piece < pieces - 1)
    def _():
        pl.semaphore_signal(barrier, inc=1, device_id={"seq": piece + 1}, device_id_type=mesh_ids)

    neighbours = jnp.where(piece > 0, 1, 0) + jnp.where(piece < pieces - 1, 1, 0)
    pl.semaphore_wait(barrier, shards - 1 + neighbours)

    def send_ids(offset):
        peer = lax.rem(me + offset, shards)
        return pltpu.make_async_remote_copy(
            src_ref=ids_ref.at[peer],
            dst_ref=ids_held.at[me],
            send_sem=ids_send_sems.at[offset],
            recv_sem=ids_recv_sems.at[me],
            device_id={"table": peer},
            device_id_type=mesh_ids,
        )

    def take_ids(source):
        return pltpu.make_async_remote_copy(
            src_ref=ids_ref.at[source],
            dst_ref=ids_held.at[source],
            send_sem=ids_send_sems.at[0],
            recv_sem=ids_recv_sems.at[source],
            device_id={"table": source},
            device_id_type=mesh_ids,
        )

    @pl.loop(1, shards)
    def _(offset):
        send_ids(offset).start()

    ids_held[me] = ids_ref[me]
    start = jnp.int32(0)
    for shard in range(shards):
        starts[shard] = start
        start = start + counts_ref[0, 0, shard]

    for first in range(0, tokens, LANES):
        ranks = order_ref[0, :, first : first + LANES]
        ranks = jnp.transpose(jnp.broadcast_to(ranks, (LANES, LANES)))
        for column in range(0, capacity, LANES):
            count = min(LANES, capacity - column)
            rank_wide[first : first + LANES, column : column + count] = ranks[:, :count]

    for part in range(parts):
        stage(part).wait()

        @pl.loop(0, part_rows, step=64)
        def _(first):
            first = pl.multiple_of(first, 64)
            target = pl.multiple_of(part * part_rows + first, 64)
            table_wide[pl.ds(target, 64)] = staged[part % slots, pl.ds(first, 64)].astype(
                jnp.float32
            )

        if part + slots < parts:
            stage(part + slots).start()

    @pl.loop(1, shards)
    def _(offset):
        take_ids(lax.rem(me + offset, shards)).wait_recv()

    to_scalar = pltpu.make_async_copy(ids_held, ids_scalar, scalar_sem)
    to_scalar.start()
    to_scalar.wait()

    def gather(peer):
        @pl.loop(0, capacity, step=16)
        def _(first):
            for i in range(16):
                row = ids_scalar[peer, 0, first + i]
                rows_wide[pl.ds(first + i, 1)] = table_wide[pl.ds(row, 1)]

        return rows_wide[...].astype(jnp.bfloat16)

    def send_rows(offset):
        peer = lax.rem(me + offset, shards)
        return pltpu.make_async_remote_copy(
            src_ref=sent.at[offset],
            dst_ref=received.at[me],
            send_sem=send_sems.at[offset],
            recv_sem=recv_sems.at[me],
            device_id={"table": peer},
            device_id_type=mesh_ids,
        )

    def take_rows(source):
        return pltpu.make_async_remote_copy(
            src_ref=sent.at[0],
            dst_ref=received.at[source],
            send_sem=send_sems.at[0],
            recv_sem=recv_sems.at[source],
            device_id={"table": source},
            device_id_type=mesh_ids,
        )

    @pl.loop(0, shards - 1)
    def _(step):
        offset = peer_offset(step, shards)
        sent[offset] = gather(lax.rem(me + offset, shards))
        send_rows(offset).start()

    received[me] = gather(me)

    def place(source, add):
        slot = lax.broadcasted_iota(jnp.int32, (1, capacity), 1)
        keys = jnp.where(slot < counts_ref[0, 0, source], starts[source] + slot, -1)

        @pl.loop(0, tokens, step=256)
        def _(first):
            at = pl.ds(pl.multiple_of(first, 256), 256)
            chosen = jnp.where(rank_wide[at] == keys, 1.0, 0.0).astype(jnp.bfloat16)
            found = jnp.dot(chosen, received[source], preferred_element_type=jnp.float32)
            found = found.astype(jnp.bfloat16)
            events[at] = events[at] + found if add else found

    place(me, False)

    @pl.loop(0, shards - 1)
    def _(step):
        source = lax.rem(me + shards - peer_offset(step, shards), shards)
        take_rows(source).wait_recv()
        place(source, True)

    @pl.loop(1, shards)
    def _(offset):
        send_ids(offset).wait_send()
        send_rows(offset).wait_send()

    load_in.wait()
    load_out.wait()
    query_scale = 0.5 * (width // HEADS) ** (-0.5)
    blocks = tokens // BLOCK
    skipped = WINDOW // BLOCK

    def block_at(block, offset=0):
        return pl.ds(pl.multiple_of(block * BLOCK + offset, BLOCK), BLOCK)

    def project(block):
        at = block_at(block)
        normed = normalize(events[at].astype(jnp.float32)).astype(jnp.bfloat16)

        def columns(first):
            weights = w_in[:, first : first + width]
            product = jnp.dot(normed, weights, preferred_element_type=jnp.float32)
            return silu_of_double(0.5 * product)

        gate[at] = columns(0).astype(gate.dtype)
        queries[at] = (columns(width) * query_scale).astype(queries.dtype)
        own = block_at(block, WINDOW)
        context[own, :width] = columns(2 * width).astype(context.dtype)
        context[own, width:] = columns(3 * width).astype(context.dtype)

    @pl.loop(blocks - skipped, blocks)
    def _(block):
        project(block)

    halo = pltpu.make_async_remote_copy(
        src_ref=context.at[pl.ds(tokens, WINDOW)],
        dst_ref=context.at[pl.ds(0, WINDOW)],
        send_sem=halo_send_sem,
        recv_sem=halo_recv_sem,
        device_id={"seq": lax.rem(piece + 1, pieces)},
        device_id_type=mesh_ids,
    )

    @pl.when(piece < pieces - 1)
    def _():
        halo.start()

    @pl.loop(0, blocks - skipped)
    def _(block):
        project(block)

    row = lax.broadcasted_iota(jnp.int32, (BLOCK, BLOCK), 0)
    column = lax.broadcasted_iota(jnp.int32, (BLOCK, BLOCK), 1)
    near = column <= row
    near_weight = near.astype(jnp.float32).astype(jnp.bfloat16)
    head_width = width // HEADS

    def attend(block):
        at = block_at(block)
        far_rows = at
        middle_rows = pl.ds(pl.multiple_of((block + 1) * BLOCK, BLOCK), WINDOW - BLOCK)
        near_rows = block_at(block, WINDOW)
        for head in range(HEADS):
            of = slice(head * head_width, (head + 1) * head_width)
            value_of = slice(width + head * head_width, width + (head + 1) * head_width)
            asked = queries[at, of]
            edge = jnp.where(
                near,
                scores_of(asked, context[near_rows, of]),
                scores_of(asked, context[far_rows, of]),
            )
            edge = silu_of_double(edge.astype(jnp.bfloat16))
            edge_near = edge * near_weight
            edge_far = edge - edge_near
            middle = silu_of_double(scores_of(asked, context[middle_rows, of]).astype(jnp.bfloat16))
            total = dot32(middle, context[middle_rows, value_of])
            total += dot32(edge_near, context[near_rows, value_of])
            total += dot32(edge_far, context[far_rows, value_of])
            heads_out[:, of] = total
        gated = normalize(heads_out[...]) * gate[at].astype(jnp.float32)
        layer = dot32(gated.astype(jnp.bfloat16), w_out[...]) + events[at].astype(jnp.float32)
        position = piece * tokens + block * BLOCK + lax.broadcasted_iota(jnp.int32, (BLOCK, 1), 0)
        result[at] = jnp.where(position < live_ref[0], layer, 0.0).astype(result.dtype)

    def write(block):
        at = block_at(block)
        return pltpu.make_async_copy(result.at[at], out_ref.at[0, at], result_sems.at[block])

    @pl.loop(skipped, blocks)
    def _(block):
        attend(block)
        write(block).start()

    @pl.when(piece > 0)
    def _():
        halo.wait_recv()

    @pl.when(piece == 0)
    def _():
        context[:WINDOW] = jnp.zeros((WINDOW, 2 * width), context.dtype)

    @pl.loop(0, skipped)
    def _(block):
        attend(block)
        write(block).start()

    @pl.when(piece < pieces - 1)
    def _():
        halo.wait_send()

    @pl.loop(0, blocks)
    def _(block):
        write(block).wait()


def local(embed_table, lookup_ids, counts, event_order, hist_len, w_uvqk, w_out):
    shards = lax.axis_size("table")
    capacity = lookup_ids.shape[3]
    tokens = event_order.shape[2]
    rows, width = embed_table.shape
    part_rows = 1024 if rows % 1024 == 0 else rows
    slots = min(2, rows // part_rows)
    kind = jnp.bfloat16
    vmem = pl.BlockSpec(memory_space=pltpu.VMEM)
    smem = pl.BlockSpec(memory_space=pltpu.SMEM)
    anywhere = pl.BlockSpec(memory_space=pl.ANY)
    dma = pltpu.SemaphoreType.DMA
    return pl.pallas_call(
        layer_kernel,
        in_specs=[vmem, smem, vmem, smem, anywhere, anywhere, anywhere],
        out_specs=anywhere,
        out_shape=jax.ShapeDtypeStruct((1, tokens, width), kind),
        scratch_shapes=[
            pltpu.VMEM((shards, 1, capacity), jnp.int32),
            pltpu.SMEM((shards,), jnp.int32),
            pltpu.VMEM((shards, 1, capacity), jnp.int32),
            pltpu.SMEM((shards, 1, capacity), jnp.int32),
            pltpu.VMEM((slots, part_rows, width), kind),
            pltpu.VMEM((rows, width), jnp.float32),
            pltpu.VMEM((tokens, capacity), jnp.int32),
            pltpu.VMEM((capacity, width), jnp.float32),
            pltpu.VMEM((shards, capacity, width), kind),
            pltpu.VMEM((shards, capacity, width), kind),
            dma((slots,)),
            dma,
            dma((shards,)),
            dma((shards,)),
            dma((shards,)),
            dma((shards,)),
            pltpu.VMEM(w_uvqk.shape, kind),
            pltpu.VMEM(w_out.shape, kind),
            dma((2,)),
            pltpu.VMEM((tokens, width), kind),
            pltpu.VMEM((tokens, width), kind),
            pltpu.VMEM((tokens, width), kind),
            pltpu.VMEM((WINDOW + tokens, 2 * width), kind),
            pltpu.VMEM((BLOCK, width), jnp.float32),
            pltpu.VMEM((tokens, width), kind),
            dma((tokens // BLOCK,)),
            dma,
            dma,
        ],
        compiler_params=pltpu.CompilerParams(
            collective_id=0, has_side_effects=True, vmem_limit_bytes=VMEM_LIMIT
        ),
        cost_estimate=pl.CostEstimate(
            flops=2 * tokens * shards * capacity * width
            + 10 * tokens * width * width
            + 4 * tokens * (WINDOW + BLOCK) * width,
            bytes_accessed=2 * rows * width + 2 * tokens * width + 10 * width * width,
            transcendentals=4 * tokens * width + tokens * WINDOW * HEADS,
        ),
        name="layer",
    )(lookup_ids, counts, event_order, hist_len, embed_table, w_uvqk, w_out)


def solution(mesh):
    in_specs = (
        P("table", None),
        P("table", "seq", None, None),
        P("table", "seq", None),
        P("table", "seq", None),
        P("table"),
        P(),
        P(),
    )
    out_specs = P("table", "seq", None)
    return jax.shard_map(local, mesh=mesh, in_specs=in_specs, out_specs=out_specs, check_vma=False)
```

time: 127 us -> 117 us (0.921)
  Pallas kernels: 119 us -> 113 us
  starting transfers between devices: 2.86 us -> 0 us
    pallas_call x4 -> x1, Pallas kernels: 119 us -> 113 us  [local(): pl.pallas_call(layer_kernel, in_specs=[vmem, smem, vmem, smem, anywhere,...]
    ppermute x1 -> x0, starting transfers between devices: 2.86 us -> none  [passed_along(): lax.ppermute(value, axis, [(source, source + steps) for source in range(i...]
    unnamed x8 -> x1, local copies, waits for them, and re-layouts: 2.91 us -> 3.05 us
  transfers between devices with their start and end apart: 1 -> 0, of which waited for: 0 -> 0; matrix products, arithmetic and copies ran while one was open for 0% -> 0% of each run, Pallas kernels for 9% -> 0%
where the time goes in v4:
time: 117 us
  Pallas kernels  113 us (97%)
  local copies, waits for them, and re-layouts  3.05 us (3%)
    pallas_call x1, Pallas kernels, local(): pl.pallas_call(layer_kernel, in_specs=[vmem, smem, vmem, smem, anywhere,...  113 us
    unnamed x1, local copies, waits for them, and re-layouts  3.05 us

profile of v4, /device:TPU:16, one launch (start us, length us, event | category | flops | bytes accessed | tf_op | source)
XLA Modules:
  0.0 116.8 jit_solution(1336435439117697910)
XLA Ops:
  0.7 113.1 %layer.1 = bf16[1,2048,512]{2,1,0:T(8,128)(2,1)} custom-call(s32[1,1,16,192]{3,2,1,0:T(8,128)} %lookup_ref.1, s32[1,1,16]{2,1,0:T(1,128)} %counts_ref.1, s32[1,1,2048]{2,1,0:T(1,128)} %order_ref.1, s32[1]{0:T(128)S(6)} %copy.9.live_ref, bf16[8192,512]{1,0:T(8,128)(2,1)} %table_ref.1, bf16[512,2048]{1,0:T(8,128)(2,1)} %w_in_ref.1, bf16[512,512]{1,0:T(8,128)(2,1)} %w_out_ref.1), custom_call_target="tpu_custom_call" | custom-call | flops 17179869184 | bytes 13107200 | tf_op jit(solution)/shard_map/layer/pallas_call | solution.py:371
  113.8 3.0 %copy.10 = bf16[1,2048,512]{2,1,0:T(8,128)(2,1)} copy(bf16[1,2048,512]{2,1,0:T(8,128)(2,1)} %layer.1) | data formatting | bytes 4194304

commit v5 on v4

--- a/solution.py
+++ b/solution.py
@@ -8,6 +8,8 @@
 HEADS = 4
 WINDOW = 1024
 BLOCK = 256
+PAIR = 2 * BLOCK
+PLACED = 1024
 LANES = 128
 VMEM_LIMIT = 60 * 1024 * 1024
 
@@ -226,9 +228,9 @@
         slot = lax.broadcasted_iota(jnp.int32, (1, capacity), 1)
         keys = jnp.where(slot < counts_ref[0, 0, source], starts[source] + slot, -1)
 
-        @pl.loop(0, tokens, step=256)
+        @pl.loop(0, tokens, step=PLACED)
         def _(first):
-            at = pl.ds(pl.multiple_of(first, 256), 256)
+            at = pl.ds(pl.multiple_of(first, PLACED), PLACED)
             chosen = jnp.where(rank_wide[at] == keys, 1.0, 0.0).astype(jnp.bfloat16)
             found = jnp.dot(chosen, received[source], preferred_element_type=jnp.float32)
             found = found.astype(jnp.bfloat16)
@@ -250,20 +252,18 @@
     load_in.wait()
     load_out.wait()
     query_scale = 0.5 * (width // HEADS) ** (-0.5)
-    blocks = tokens // BLOCK
-    skipped = WINDOW // BLOCK
-
-    def block_at(block, offset=0):
-        return pl.ds(pl.multiple_of(block * BLOCK + offset, BLOCK), BLOCK)
+    blocks = tokens // PAIR
+    skipped = WINDOW // PAIR
+
+    def block_at(block, offset=0, count=PAIR):
+        return pl.ds(pl.multiple_of(block * PAIR + offset, BLOCK), count)
 
     def project(block):
         at = block_at(block)
-        normed = normalize(events[at].astype(jnp.float32)).astype(jnp.bfloat16)
+        normed = (0.5 * normalize(events[at].astype(jnp.float32))).astype(jnp.bfloat16)
 
         def columns(first):
-            weights = w_in[:, first : first + width]
-            product = jnp.dot(normed, weights, preferred_element_type=jnp.float32)
-            return silu_of_double(0.5 * product)
+            return silu_of_double(dot32(normed, w_in[:, first : first + width]))
 
         gate[at] = columns(0).astype(gate.dtype)
         queries[at] = (columns(width) * query_scale).astype(queries.dtype)
@@ -300,29 +300,39 @@
 
     def attend(block):
         at = block_at(block)
-        far_rows = at
-        middle_rows = pl.ds(pl.multiple_of((block + 1) * BLOCK, BLOCK), WINDOW - BLOCK)
-        near_rows = block_at(block, WINDOW)
+        oldest = block_at(block, 0, BLOCK)
+        newest = block_at(block, WINDOW + BLOCK, BLOCK)
+        shared = block_at(block, BLOCK, WINDOW)
         for head in range(HEADS):
             of = slice(head * head_width, (head + 1) * head_width)
             value_of = slice(width + head * head_width, width + (head + 1) * head_width)
             asked = queries[at, of]
-            edge = jnp.where(
-                near,
-                scores_of(asked, context[near_rows, of]),
-                scores_of(asked, context[far_rows, of]),
+            whole = scores_of(asked, context[shared, of])
+            upper_far = scores_of(asked[:BLOCK], context[oldest, of])
+            lower_near = scores_of(asked[BLOCK:], context[newest, of])
+            upper_edge = jnp.where(near, whole[:BLOCK, WINDOW - BLOCK :], upper_far)
+            lower_edge = jnp.where(near, lower_near, whole[BLOCK:, :BLOCK])
+            upper_edge = silu_of_double(upper_edge.astype(jnp.bfloat16))
+            lower_edge = silu_of_double(lower_edge.astype(jnp.bfloat16))
+            upper_near = upper_edge * near_weight
+            lower_near = lower_edge * near_weight
+            upper = silu_of_double(whole[:BLOCK, : WINDOW - BLOCK].astype(jnp.bfloat16))
+            lower = silu_of_double(whole[BLOCK:, BLOCK:].astype(jnp.bfloat16))
+            weights = jnp.concatenate(
+                [
+                    jnp.concatenate([upper, upper_near], axis=1),
+                    jnp.concatenate([lower_edge - lower_near, lower], axis=1),
+                ],
+                axis=0,
             )
-            edge = silu_of_double(edge.astype(jnp.bfloat16))
-            edge_near = edge * near_weight
-            edge_far = edge - edge_near
-            middle = silu_of_double(scores_of(asked, context[middle_rows, of]).astype(jnp.bfloat16))
-            total = dot32(middle, context[middle_rows, value_of])
-            total += dot32(edge_near, context[near_rows, value_of])
-            total += dot32(edge_far, context[far_rows, value_of])
-            heads_out[:, of] = total
+            total = dot32(weights, context[shared, value_of])
+            heads_out[:BLOCK, of] = total[:BLOCK] + dot32(
+                upper_edge - upper_near, context[oldest, value_of]
+            )
+            heads_out[BLOCK:, of] = total[BLOCK:] + dot32(lower_near, context[newest, value_of])
         gated = normalize(heads_out[...]) * gate[at].astype(jnp.float32)
         layer = dot32(gated.astype(jnp.bfloat16), w_out[...]) + events[at].astype(jnp.float32)
-        position = piece * tokens + block * BLOCK + lax.broadcasted_iota(jnp.int32, (BLOCK, 1), 0)
+        position = piece * tokens + block * PAIR + lax.broadcasted_iota(jnp.int32, (PAIR, 1), 0)
         result[at] = jnp.where(position < live_ref[0], layer, 0.0).astype(result.dtype)
 
     def write(block):
@@ -362,7 +372,7 @@
     tokens = event_order.shape[2]
     rows, width = embed_table.shape
     part_rows = 1024 if rows % 1024 == 0 else rows
-    slots = min(2, rows // part_rows)
+    slots = min(4, rows // part_rows)
     kind = jnp.bfloat16
     vmem = pl.BlockSpec(memory_space=pltpu.VMEM)
     smem = pl.BlockSpec(memory_space=pltpu.SMEM)
@@ -397,9 +407,9 @@
             pltpu.VMEM((tokens, width), kind),
             pltpu.VMEM((tokens, width), kind),
             pltpu.VMEM((WINDOW + tokens, 2 * width), kind),
-            pltpu.VMEM((BLOCK, width), jnp.float32),
+            pltpu.VMEM((PAIR, width), jnp.float32),
             pltpu.VMEM((tokens, width), kind),
-            dma((tokens // BLOCK,)),
+            dma((tokens // PAIR,)),
             dma,
             dma,
         ],

time: 117 us -> 108 us (0.923)
  Pallas kernels: 113 us -> 104 us
    pallas_call x1, Pallas kernels: 113 us -> 104 us  [local(): pl.pallas_call(layer_kernel, in_specs=[vmem, smem, vmem, smem, anywhere,...]
where the time goes in v5:
time: 108 us; the launch traced here: 107 us
  Pallas kernels  104 us (96%)
  local copies, waits for them, and re-layouts  3.05 us (3%)
    pallas_call x1, Pallas kernels, local(): pl.pallas_call(layer_kernel, in_specs=[vmem, smem, vmem, smem, anywhere,...  104 us
    unnamed x1, local copies, waits for them, and re-layouts  3.05 us

profile of v5, /device:TPU:16, one launch (start us, length us, event | category | flops | bytes accessed | tf_op | source)
XLA Modules:
  0.0 107.3 jit_solution(6331755071293809192)
XLA Ops:
  0.7 103.6 %layer.1 = bf16[1,2048,512]{2,1,0:T(8,128)(2,1)} custom-call(s32[1,1,16,192]{3,2,1,0:T(8,128)} %lookup_ref.1, s32[1,1,16]{2,1,0:T(1,128)} %counts_ref.1, s32[1,1,2048]{2,1,0:T(1,128)} %order_ref.1, s32[1]{0:T(128)S(6)} %copy.9.live_ref, bf16[8192,512]{1,0:T(8,128)(2,1)} %table_ref.1, bf16[512,2048]{1,0:T(8,128)(2,1)} %w_in_ref.1, bf16[512,512]{1,0:T(8,128)(2,1)} %w_out_ref.1), custom_call_target="tpu_custom_call" | custom-call | flops 17179869184 | bytes 13107200 | tf_op jit(solution)/shard_map/layer/pallas_call | solution.py:381
  104.3 3.0 %copy.10 = bf16[1,2048,512]{2,1,0:T(8,128)(2,1)} copy(bf16[1,2048,512]{2,1,0:T(8,128)(2,1)} %layer.1) | data formatting | bytes 4194304

commit v6 on v5

--- a/solution.py
+++ b/solution.py
@@ -9,7 +9,7 @@
 WINDOW = 1024
 BLOCK = 256
 PAIR = 2 * BLOCK
-PLACED = 1024
+PLACED = 2048
 LANES = 128
 VMEM_LIMIT = 60 * 1024 * 1024
 
@@ -228,9 +228,8 @@
         slot = lax.broadcasted_iota(jnp.int32, (1, capacity), 1)
         keys = jnp.where(slot < counts_ref[0, 0, source], starts[source] + slot, -1)
 
-        @pl.loop(0, tokens, step=PLACED)
-        def _(first):
-            at = pl.ds(pl.multiple_of(first, PLACED), PLACED)
+        for first in range(0, tokens, PLACED):
+            at = slice(first, first + PLACED)
             chosen = jnp.where(rank_wide[at] == keys, 1.0, 0.0).astype(jnp.bfloat16)
             found = jnp.dot(chosen, received[source], preferred_element_type=jnp.float32)
             found = found.astype(jnp.bfloat16)
@@ -256,23 +255,23 @@
     skipped = WINDOW // PAIR
 
     def block_at(block, offset=0, count=PAIR):
-        return pl.ds(pl.multiple_of(block * PAIR + offset, BLOCK), count)
+        first = block * PAIR + offset
+        return pl.ds(first if isinstance(first, int) else pl.multiple_of(first, BLOCK), count)
 
     def project(block):
         at = block_at(block)
         normed = (0.5 * normalize(events[at].astype(jnp.float32))).astype(jnp.bfloat16)
 
-        def columns(first):
-            return silu_of_double(dot32(normed, w_in[:, first : first + width]))
-
-        gate[at] = columns(0).astype(gate.dtype)
-        queries[at] = (columns(width) * query_scale).astype(queries.dtype)
+        def columns(first, kind):
+            return silu_of_double(dot32(normed, w_in[:, first : first + width]).astype(kind))
+
+        gate[at] = columns(0, jnp.float32).astype(gate.dtype)
+        queries[at] = (columns(width, jnp.bfloat16).astype(jnp.float32) * query_scale).astype(queries.dtype)
         own = block_at(block, WINDOW)
-        context[own, :width] = columns(2 * width).astype(context.dtype)
-        context[own, width:] = columns(3 * width).astype(context.dtype)
-
-    @pl.loop(blocks - skipped, blocks)
-    def _(block):
+        context[own, :width] = columns(2 * width, context.dtype)
+        context[own, width:] = columns(3 * width, context.dtype)
+
+    for block in range(blocks - skipped, blocks):
         project(block)
 
     halo = pltpu.make_async_remote_copy(
@@ -288,8 +287,7 @@
     def _():
         halo.start()
 
-    @pl.loop(0, blocks - skipped)
-    def _(block):
+    for block in range(blocks - skipped):
         project(block)
 
     row = lax.broadcasted_iota(jnp.int32, (BLOCK, BLOCK), 0)

time: 108 us -> 107 us (level)
  no operation moved by 1% of the time
where the time goes in v6:
time: 107 us; the launch traced here: 106 us
  Pallas kernels  103 us (96%)
  local copies, waits for them, and re-layouts  3.05 us (3%)
    pallas_call x1, Pallas kernels, local(): pl.pallas_call(layer_kernel, in_specs=[vmem, smem, vmem, smem, anywhere,...  103 us
    unnamed x1, local copies, waits for them, and re-layouts  3.05 us

profile of v6, /device:TPU:16, one launch (start us, length us, event | category | flops | bytes accessed | tf_op | source)
XLA Modules:
  0.0 106.5 jit_solution(12935221356146633171)
XLA Ops:
  0.7 102.8 %layer.1 = bf16[1,2048,512]{2,1,0:T(8,128)(2,1)} custom-call(s32[1,1,16,192]{3,2,1,0:T(8,128)} %lookup_ref.1, s32[1,1,16]{2,1,0:T(1,128)} %counts_ref.1, s32[1,1,2048]{2,1,0:T(1,128)} %order_ref.1, s32[1]{0:T(128)S(6)} %copy.9.live_ref, bf16[8192,512]{1,0:T(8,128)(2,1)} %table_ref.1, bf16[512,2048]{1,0:T(8,128)(2,1)} %w_in_ref.1, bf16[512,512]{1,0:T(8,128)(2,1)} %w_out_ref.1), custom_call_target="tpu_custom_call" | custom-call | flops 17179869184 | bytes 13107200 | tf_op jit(solution)/shard_map/layer/pallas_call | solution.py:379
  103.5 3.0 %copy.10 = bf16[1,2048,512]{2,1,0:T(8,128)(2,1)} copy(bf16[1,2048,512]{2,1,0:T(8,128)(2,1)} %layer.1) | data formatting | bytes 4194304

commit v7 on v6

--- a/solution.py
+++ b/solution.py
@@ -296,12 +296,14 @@
     near_weight = near.astype(jnp.float32).astype(jnp.bfloat16)
     head_width = width // HEADS
 
-    def attend(block):
+    def attend(block, held, between):
         at = block_at(block)
         oldest = block_at(block, 0, BLOCK)
         newest = block_at(block, WINDOW + BLOCK, BLOCK)
         shared = block_at(block, BLOCK, WINDOW)
         for head in range(HEADS):
+            if head == 1:
+                between()
             of = slice(head * head_width, (head + 1) * head_width)
             value_of = slice(width + head * head_width, width + (head + 1) * head_width)
             asked = queries[at, of]
@@ -324,11 +326,14 @@
                 axis=0,
             )
             total = dot32(weights, context[shared, value_of])
-            heads_out[:BLOCK, of] = total[:BLOCK] + dot32(
+            heads_out[held, :BLOCK, of] = total[:BLOCK] + dot32(
                 upper_edge - upper_near, context[oldest, value_of]
             )
-            heads_out[BLOCK:, of] = total[BLOCK:] + dot32(lower_near, context[newest, value_of])
-        gated = normalize(heads_out[...]) * gate[at].astype(jnp.float32)
+            heads_out[held, BLOCK:, of] = total[BLOCK:] + dot32(lower_near, context[newest, value_of])
+
+    def finish(block, held):
+        at = block_at(block)
+        gated = normalize(heads_out[held]) * gate[at].astype(jnp.float32)
         layer = dot32(gated.astype(jnp.bfloat16), w_out[...]) + events[at].astype(jnp.float32)
         position = piece * tokens + block * PAIR + lax.broadcasted_iota(jnp.int32, (PAIR, 1), 0)
         result[at] = jnp.where(position < live_ref[0], layer, 0.0).astype(result.dtype)
@@ -337,11 +342,21 @@
         at = block_at(block)
         return pltpu.make_async_copy(result.at[at], out_ref.at[0, at], result_sems.at[block])
 
-    @pl.loop(skipped, blocks)
-    def _(block):
-        attend(block)
+    def write_finished(block, held):
+        finish(block, held)
         write(block).start()
 
+    order = [*range(skipped, blocks), *range(skipped)]
+
+    def attend_turns(first, last):
+        for turn in range(first, last):
+            between = lambda: None
+            if turn > 0:
+                between = lambda: write_finished(order[turn - 1], (turn - 1) % 2)
+            attend(order[turn], turn % 2, between)
+
+    attend_turns(0, blocks - skipped)
+
     @pl.when(piece > 0)
     def _():
         halo.wait_recv()
@@ -350,10 +365,8 @@
     def _():
         context[:WINDOW] = jnp.zeros((WINDOW, 2 * width), context.dtype)
 
-    @pl.loop(0, skipped)
-    def _(block):
-        attend(block)
-        write(block).start()
+    attend_turns(blocks - skipped, blocks)
+    write_finished(order[-1], (blocks - 1) % 2)
 
     @pl.when(piece < pieces - 1)
     def _():
@@ -405,7 +418,7 @@
             pltpu.VMEM((tokens, width), kind),
             pltpu.VMEM((tokens, width), kind),
             pltpu.VMEM((WINDOW + tokens, 2 * width), kind),
-            pltpu.VMEM((PAIR, width), jnp.float32),
+            pltpu.VMEM((2, PAIR, width), jnp.float32),
             pltpu.VMEM((tokens, width), kind),
             dma((tokens // PAIR,)),
             dma,

time: 107 us -> 105 us (0.981)
  Pallas kernels: 103 us -> 101 us
    pallas_call x1, Pallas kernels: 103 us -> 101 us  [local(): pl.pallas_call(layer_kernel, in_specs=[vmem, smem, vmem, smem, anywhere,...]
where the time goes in v7:
time: 105 us
  Pallas kernels  101 us (96%)
  local copies, waits for them, and re-layouts  3.05 us (3%)
    pallas_call x1, Pallas kernels, local(): pl.pallas_call(layer_kernel, in_specs=[vmem, smem, vmem, smem, anywhere,...  101 us
    unnamed x1, local copies, waits for them, and re-layouts  3.05 us

profile of v7, /device:TPU:16, one launch (start us, length us, event | category | flops | bytes accessed | tf_op | source)
XLA Modules:
  0.0 105.1 jit_solution(8335490084924677654)
XLA Ops:
  0.7 101.4 %layer.1 = bf16[1,2048,512]{2,1,0:T(8,128)(2,1)} custom-call(s32[1,1,16,192]{3,2,1,0:T(8,128)} %lookup_ref.1, s32[1,1,16]{2,1,0:T(1,128)} %counts_ref.1, s32[1,1,2048]{2,1,0:T(1,128)} %order_ref.1, s32[1]{0:T(128)S(6)} %copy.9.live_ref, bf16[8192,512]{1,0:T(8,128)(2,1)} %table_ref.1, bf16[512,2048]{1,0:T(8,128)(2,1)} %w_in_ref.1, bf16[512,512]{1,0:T(8,128)(2,1)} %w_out_ref.1), custom_call_target="tpu_custom_call" | custom-call | flops 17179869184 | bytes 13107200 | tf_op jit(solution)/shard_map/layer/pallas_call | solution.py:392
  102.1 3.0 %copy.10 = bf16[1,2048,512]{2,1,0:T(8,128)(2,1)} copy(bf16[1,2048,512]{2,1,0:T(8,128)(2,1)} %layer.1) | data formatting | bytes 4194304
